TPU v7x, 256 devices: a whole 4x4x8 slice. The times are simulated.
256 devices in a mesh: ctx: 64 (over x, z, core), tp: 4 (over y).
Axes of the slice: x: 4, y: 4, z: 8, core: 2. Of those that a mesh axis runs over, the one named last changes fastest.
Arguments:
- queries: bfloat16 [32768, 8192], P('ctx', 'tp')
- keys: bfloat16 [32768, 1024], P('ctx', 'tp')
- values: bfloat16 [32768, 1024], P('ctx', 'tp'), may hold values from -6 to 6
- block_lengths: int32 [64], replicated, may hold values from 256 to 512, as said below
- decode_query_rows: bfloat16 [64, 8192], P('ctx', 'tp')
- out_weight: bfloat16 [8192, 8192], P('tp', 'ctx'), may hold values from -0.0625 to 0.0625
Outputs:
- block_out: bfloat16 [32768, 8192], P('ctx', 'tp')
- decode_out: bfloat16 [64, 8192], P(None, 'ctx')
Inputs may be any that keep to these rules, and one draw needn't show every extreme that they name: `block_lengths`: each block has between 256 and 512 live slots, at its lowest offsets; in every draw some block is full.
All inputs are finite; a program needn't handle non-finite values.
Results may differ from a plain program's by a relative error of at most 0.0056.
Values may be sent and summed in bfloat16 or wider, within the bound.
No kernel may reach another device: no remote copies, remote signals or barrier semaphores. Data moves between devices by JAX's collectives and lax.ppermute only.
A program may use at most 192 MiB of HBM per device.

v0:
```python
import jax
import jax.numpy as jnp
from jax import lax
from jax.sharding import PartitionSpec as P

HEAD_SIZE = 128


def broadcast(block, axis, owner):
    block = jnp.where(lax.axis_index(axis) == owner, block, jnp.zeros_like(block))
    return lax.psum(block, axis)


def fetch_anchor(keys, values):
    return broadcast(jnp.stack([keys, values]), "ctx", 0)


def body(queries, keys, values, block_lengths, decode_query_rows, out_weight):
    row_count = queries.shape[0]
    kv_local = keys.shape[1] // HEAD_SIZE
    group_width = queries.shape[1] // keys.shape[1]
    inv_root = HEAD_SIZE ** (-0.5)
    block_index = lax.axis_index("ctx")
    own_len = block_lengths[block_index]
    anchor_len = block_lengths[0]
    query_heads = queries.reshape(row_count, kv_local, group_width, HEAD_SIZE)
    key_heads = keys.reshape(row_count, kv_local, HEAD_SIZE)
    value_heads = values.reshape(row_count, kv_local, HEAD_SIZE)
    offsets = jnp.arange(row_count, dtype=jnp.int32)
    anchor_ok = (offsets < anchor_len) & (block_index > 0)
    own_ok = (offsets[None, :] <= offsets[:, None]) & (offsets[None, :] < own_len)

    def score_with(key_part):
        return (
            jnp.einsum("ikgd,jkd->kgij", query_heads, key_part, preferred_element_type=jnp.float32)
            * inv_root
        )

    anchor = fetch_anchor(keys, values)
    anchor_scores = score_with(anchor[0].reshape(row_count, kv_local, HEAD_SIZE))
    own_scores = score_with(key_heads)
    scores = jnp.concatenate(
        [jnp.where(anchor_ok, anchor_scores, -1e30), jnp.where(own_ok, own_scores, -1e30)], axis=-1
    )
    top_score = jnp.max(scores, axis=-1, keepdims=True)
    powers = jnp.exp(scores - top_score)
    totals = jnp.sum(powers, axis=-1)
    shares = powers.astype(jnp.bfloat16)
    value_cat = jnp.concatenate(
        [anchor[1].reshape(row_count, kv_local, HEAD_SIZE), value_heads], axis=0
    )
    weighted = jnp.einsum("kgij,jkd->ikgd", shares, value_cat, preferred_element_type=jnp.float32)
    result = weighted / jnp.transpose(totals, (2, 0, 1))[..., None]
    result = jnp.where((offsets < own_len)[:, None, None, None], result, 0.0)
    block_out = result.reshape(row_count, kv_local * group_width * HEAD_SIZE).astype(jnp.bfloat16)
    decode_all = lax.all_gather(decode_query_rows, "ctx", axis=0, tiled=True)
    decode_count = decode_all.shape[0]
    decode_heads = decode_all.reshape(decode_count, kv_local, group_width, HEAD_SIZE)
    dec_scores = (
        jnp.einsum("rkgd,jkd->kgrj", decode_heads, key_heads, preferred_element_type=jnp.float32)
        * inv_root
    )
    dec_scores = jnp.where(offsets < own_len, dec_scores, -1e30)
    dec_top = jnp.max(dec_scores, axis=-1)
    dec_powers = jnp.exp(dec_scores - dec_top[..., None])
    dec_totals = jnp.sum(dec_powers, axis=-1)
    dec_shares = dec_powers.astype(jnp.bfloat16)
    dec_weighted = jnp.einsum(
        "kgrj,jkd->kgrd", dec_shares, value_heads, preferred_element_type=jnp.float32
    )
    overall = lax.pmax(dec_top, "ctx")
    factors = jnp.exp(dec_top - overall)
    total_sum, weighted_sum = lax.psum(
        (dec_totals * factors, dec_weighted * factors[..., None]), "ctx"
    )
    attn = (
        jnp.transpose(weighted_sum / total_sum[..., None], (2, 0, 1, 3))
        .reshape(decode_count, kv_local * group_width * HEAD_SIZE)
        .astype(jnp.bfloat16)
    )
    projected = jnp.dot(attn, out_weight, preferred_element_type=jnp.float32)
    decode_out = lax.psum(projected, "tp").astype(jnp.bfloat16)
    return (block_out, decode_out)


def solution(mesh):
    return jax.shard_map(
        body,
        mesh=mesh,
        in_specs=(
            P("ctx", "tp"),
            P("ctx", "tp"),
            P("ctx", "tp"),
            P(),
            P("ctx", "tp"),
            P("tp", "ctx"),
        ),
        out_specs=(P("ctx", "tp"), P(None, "ctx")),
        check_vma=False,
    )
```

profile of v0, /device:TPU:1, one launch (start us, length us, event | category | flops | bytes accessed | tf_op | source)
XLA Modules:
  0.0 596.0 jit_solution(12296573058833885838)
XLA Ops:
  7.2 0.0 copy-start
  7.2 0.0 all-reduce.5.cloned.1.call-start
  7.2 1.3 fusion.37
  8.5 0.6 iota_compare_fusion.2
  9.2 1.1 copy.31
  10.3 1.0 reshape.40
  11.3 54.7 %all-gather = bf16[64,1,2048]{2,1,0:T(2,128)(2,1)S(1)} all-gather(bf16[1,1,2048]{2,1,0:T(2,128)(2,1)} %bitcast.77), channel_id=1, replica_groups=mesh['ctx'=64,'tp'=4] {'ctx'}, dimensions={0}, use_global_device_ids=true | all-gather | bytes 266240 | tf_op jit(solution)/shard_map/all_gather | solution.py:56
  66.0 1.5 reduce.2
  67.5 0.0 copy-start.2
  67.6 0.5 bitcast_reduce_fusion
  68.1 125.6 %pmax.7 = f32[2,8,64]{2,1,0:T(8,128)S(1)} all-reduce(f32[2,8,64]{2,1,0:T(8,128)S(1)} %get-tuple-element.18), channel_id=1, replica_groups=mesh['ctx'=64,'tp'=4] {'ctx'}, use_global_device_ids=true, to_apply=%region_5.6 | all-reduce | flops 1024 | bytes 8192 | tf_op jit(solution)/shard_map/pmax | solution.py:71
  193.7 0.6 fusion.12
  194.3 1.5 convolution_multiply_fusion
  195.8 0.0 all-reduce.5.cloned.1.call-update
  195.8 0.0 all-reduce.3.cloned.1.call-start
  195.8 0.0 copy-done.2
  195.9 0.1 copy.30
  196.0 0.9 maximum_select_fusion
  196.9 0.0 all-reduce.3.cloned.1.call-update
  196.9 0.1 fusion.18
  197.0 128.8 %psum.30 = f32[2,8,64]{2,1,0:T(8,128)S(1)} all-reduce(f32[2,8,64]{2,1,0:T(8,128)S(1)} %get-tuple-element.8), channel_id=1, replica_groups=mesh['ctx'=64,'tp'=4] {'ctx'}, use_global_device_ids=true, to_apply=%region_8.9 | all-reduce | flops 1024 | bytes 8192 | tf_op jit(solution)/shard_map/psum | solution.py:73
  325.8 2.2 copy.57
  328.1 0.7 fusion.30
  328.7 7.6 %fusion.39 = (f32[2,8,512]{2,1,0:T(8,128)S(1)}, f32[2,8,512,512]{2,3,1,0:T(8,128)}) fusion(bf16[512,2,8,128]{3,2,1,0:T(8,128)(2,1)S(1)} %bitcast.61, bf16[512,2,128,1]{2,1,0,3:T(2,128)(2,1)S(1)} %bitcast.64, pred[512,512]{0,1:T(8,128)(4,1)S(1)} %fusion.18), kind=kOutput, calls=%fused_computation.50 | convolution fusion | flops 1086316544 | bytes 19431424 | tf_op jit(solution)/shard_map/ikgd,jkd->kgij/dot_general | solution.py:35
  336.3 35.8 %all-reduce.5.cloned.1.call-done = f32[2,8,64,128]{3,2,1,0:T(8,128)} async-done(((f32[2,8,64,128]{3,2,1,0:T(8,128)}), f32[2,8,64,128]{3,2,1,0:T(8,128)}) %all-reduce.5.cloned.1.call-update) | async-done | bytes 524304 | tf_op jit(solution)/shard_map/psum | solution.py:73
  372.0 1.2 fusion.27
  373.3 0.2 copy.41
  373.5 0.0 copy-done
  373.5 0.2 fusion.22
  373.7 13.9 %psum.31 = bf16[64,128]{1,0:T(8,128)(2,1)} all-reduce(f32[64,128]{1,0:T(8,128)S(1)} %fusion.22), channel_id=1, replica_groups=mesh['ctx'=64,'tp'=4] {'tp'}, use_global_device_ids=true, to_apply=%region_9.10 | all-reduce | flops 8192 | bytes 49152 | tf_op jit(solution)/shard_map/psum | solution.py:82
  387.6 167.4 %all-reduce.3.cloned.1.call-done = bf16[2,512,256]{1,2,0:T(8,128)(2,1)} async-done(((bf16[2,512,256]{1,2,0:T(8,128)(2,1)}), bf16[2,512,256]{1,2,0:T(8,128)(2,1)}) %all-reduce.3.cloned.1.call-update) | async-done | bytes 524304 | tf_op jit(solution)/shard_map/psum | solution.py:11
  555.0 1.1 fusion.36
  556.1 0.0 copy-start.1
  556.1 10.6 %fusion.38 = (f32[2,8,512]{2,1,0:T(8,128)S(1)}, f32[2,8,512,512]{2,3,1,0:T(8,128)}) fusion(bf16[512,2,128,1]{0,2,3,1:T(8,128)(2,1)S(1)} %bitcast.67, bf16[512,2,8,128]{3,2,1,0:T(8,128)(2,1)S(1)} %bitcast.62, pred[512]{0:T(512)(128)(4,1)S(1)} %fusion.30), kind=kOutput, calls=%fused_computation.49 | convolution fusion | flops 1086316544 | bytes 19169792 | tf_op jit(solution)/shard_map/ikgd,jkd->kgij/dot_general | solution.py:35
  566.6 0.7 copy-done.1
  567.3 9.9 %fusion.1 = f32[2,8,512]{2,1,0:T(8,128)S(1)} fusion(f32[2,8,512,512]{2,3,1,0:T(8,128)S(1)} %copy-done.1, f32[2,8,512,512]{2,3,1,0:T(8,128)} %get-tuple-element.15, f32[2,8,512]{2,1,0:T(8,128)S(1)} %reduce_max.31), kind=kLoop, calls=%fused_computation.2 | loop fusion | flops 25157632 | bytes 33619968 | tf_op jit(solution)/shard_map/reduce_sum | solution.py:47
  577.2 9.5 %fusion.6 = bf16[512,2,8,128]{0,3,2,1:T(8,128)(2,1)S(1)} fusion(f32[2,8,512,512]{2,3,1,0:T(8,128)S(1)} %copy-done.1, f32[2,8,512,512]{2,3,1,0:T(8,128)} %get-tuple-element.15, f32[2,8,512]{2,1,0:T(8,128)S(1)} %reduce_max.31, f32[512,2,8]{0,2,1:T(8,128)S(1)} %bitcast.76, pred[512]{0:T(512)(128)(4,1)S(1)} %iota_compare_fusion.2, ...), kind=kOutput, calls=%fused_computation.9 | convolution fusion | flops 2176843776 | bytes 36241920 | tf_op jit(solution)/shard_map/kgij,jkd->ikgd/dot_general | solution.py:52
  586.8 2.4 copy.42
  (3 shorter events, 0.1 us)
Async XLA Ops:
  7.2 366.3 %copy-start = (bf16[2048,128]{1,0:T(8,128)(2,1)S(1)}, bf16[2048,128]{1,0:T(8,128)(2,1)}, u32[]{:S(2)}) copy-start(bf16[2048,128]{1,0:T(8,128)(2,1)} %param.11) | copy-start | bytes 1572868
  7.2 364.9 %all-reduce.5.cloned.1.call-start = ((), (), s32[]{:S(2)}) async-start(), calls=%async_computation.1 | async-start | bytes 1048576 | tf_op jit(solution)/shard_map/psum | solution.py:73
  67.5 128.3 %copy-start.2 = (bf16[512,256]{1,0:T(8,128)(2,1)S(1)}, bf16[512,256]{1,0:T(8,128)(2,1)}, u32[]{:S(2)}) copy-start(bf16[512,256]{1,0:T(8,128)(2,1)} %param.7) | copy-start | bytes 786436
  195.8 359.2 %all-reduce.3.cloned.1.call-start = ((), (), s32[]{:S(2)}) async-start(), calls=%async_computation | async-start | bytes 1048576 | tf_op jit(solution)/shard_map/psum | solution.py:11
  556.1 11.2 %copy-start.1 = (f32[2,8,512,512]{2,3,1,0:T(8,128)S(1)}, f32[2,8,512,512]{2,3,1,0:T(8,128)}, u32[]{:S(2)}) copy-start(f32[2,8,512,512]{2,3,1,0:T(8,128)} %get-tuple-element.17) | copy-start | bytes 50331652
Sparse Core Ops, SparseCore 0:
  195.9 176.0 all-reduce.4
  376.1 178.8 all-reduce.2
where the time goes:
time: 597 us; the launch traced here: 596 us
  blocking collectives  323 us (54%)
  waiting for transfers between devices  203 us (34%)
  matrix products  29.9 us (5%)
  other arithmetic  15.6 us (3%)
  between operations  14.2 us (2%)
  local copies, waits for them, and re-layouts  10.1 us (2%)
    psum x1, waiting for transfers between devices, broadcast(): return lax.psum(block, axis)  167 us
    psum x1, blocking collectives, body(): lax.psum((dec_totals * factors, dec_weighted * factors[..., None]), 'ctx')  129 us
    pmax x1, blocking collectives, body(): overall = lax.pmax(dec_top, 'ctx')  126 us
    all_gather x1, blocking collectives, body(): decode_all = lax.all_gather(decode_query_rows, 'ctx', axis=0, tiled=True)  54.7 us
    psum x1, waiting for transfers between devices, body(): lax.psum((dec_totals * factors, dec_weighted * factors[..., None]), 'ctx')  35.8 us
    dot_general x2, matrix products, score_with(): jnp.einsum('ikgd,jkd->kgij', query_heads, key_part, preferred_element_typ...  18.1 us
    psum x1, blocking collectives, body(): decode_out = lax.psum(projected, 'tp').astype(jnp.bfloat16)  13.9 us
  transfers between devices with their start and end apart: 2, of which 2 were waited for; matrix products, arithmetic and copies ran while one was open for 2% of the time, Pallas kernels for 0%

commit v1 on v0

v1 whole, which is shorter than its diff:
```python
import functools
import math

import jax
import jax.numpy as jnp
from jax import lax
from jax.experimental import pallas as pl
from jax.experimental.pallas import tpu as pltpu
from jax.sharding import PartitionSpec as P

HEAD = 128
GROUP = 8
KV = 2
SLOTS = 512
HALF = 256
ROWS = 64
NX, NZ, NCORE, NTP = 4, 8, 2, 4
WIDE = KV * GROUP * HEAD
MESSAGE = WIDE + 128
EXP2_SCALE = HEAD**-0.5 * math.log2(math.e)
NEG = -1e30
NT = (((1,), (1,)), ((), ()))


def ctx_at(x, z, core):
    return (x * NZ + z) * NCORE + core


XC_GROUPS = [[ctx_at(x, z, c) for x in range(NX) for c in range(NCORE)] for z in range(NZ)]
Z_GROUPS = [[ctx_at(x, z, c) for z in range(NZ)] for x in range(NX) for c in range(NCORE)]


def qk(q, k):
    return lax.dot_general(q, k, NT, preferred_element_type=jnp.float32)


def pv(p, v):
    return jnp.dot(p.astype(jnp.bfloat16), v, preferred_element_type=jnp.float32)


def block_kernel(info, q_ref, k_ref, v_ref, one_ref, two_ref, *rest):
    o_ref = rest[-1]
    own_len, anchor_len, core = info[0], info[1], info[2]
    one, two = one_ref[...], two_ref[...]
    ka = jnp.where(core == 0, one, two)
    va = jnp.where(core == 0, two, one)
    lane = lax.broadcasted_iota(jnp.int32, (HALF, HALF), 1)
    row = lax.broadcasted_iota(jnp.int32, (HALF, HALF), 0)
    for part in range(2):
        rows = pl.ds(part * HALF, HALF)
        q = q_ref[rows, :]
        own = qk(q, k_ref[: HALF * (part + 1), :])
        anchor = qk(q, ka)
        pieces = [
            jnp.where(lane < anchor_len, anchor[:, :HALF], NEG),
            jnp.where(lane + HALF < anchor_len, anchor[:, HALF:], NEG),
        ]
        if part:
            pieces.append(own[:, :HALF])
        pieces.append(jnp.where(lane <= row, own[:, part * HALF :], NEG))
        scores = jnp.concatenate(pieces, axis=1)
        top = jnp.max(scores, axis=1, keepdims=True)
        powers = jnp.exp2((scores - top) * EXP2_SCALE)
        total = jnp.sum(powers, axis=1, keepdims=True)
        weighted = pv(powers[:, :SLOTS], va) + pv(powers[:, SLOTS:], v_ref[: HALF * (part + 1), :])
        live = lax.broadcasted_iota(jnp.int32, (HALF, HEAD), 0) + part * HALF < own_len
        o_ref[rows, :] = jnp.where(live, weighted / total, 0.0).astype(o_ref.dtype)


def block_pass(kv, info, queries, keys, values, one, two, out):
    head = lambda g, info: (0, kv * GROUP + g)
    shared = lambda g, info: (0, kv)
    specs = [pl.BlockSpec((SLOTS, HEAD), head)] + [pl.BlockSpec((SLOTS, HEAD), shared)] * 4
    operands = [queries, keys, values, one, two]
    aliases = {}
    if out is not None:
        specs.append(pl.BlockSpec(memory_space=pl.ANY))
        operands.append(out)
        aliases = {6: 0}
    return pl.pallas_call(
        block_kernel,
        grid_spec=pltpu.PrefetchScalarGridSpec(
            num_scalar_prefetch=1,
            grid=(GROUP,),
            in_specs=specs,
            out_specs=pl.BlockSpec((SLOTS, HEAD), head),
        ),
        out_shape=jax.ShapeDtypeStruct(queries.shape, jnp.bfloat16),
        input_output_aliases=aliases,
        compiler_params=pltpu.CompilerParams(vmem_limit_bytes=32 << 20),
        cost_estimate=pl.CostEstimate(
            flops=GROUP * SLOTS * SLOTS * HEAD * 8, bytes_accessed=4 << 20, transcendentals=GROUP * SLOTS * 1024
        ),
        name="block_pass",
    )(info, *operands)


def pack_lse(lse):
    lane = lax.broadcasted_iota(jnp.int32, lse.shape, 1)
    high = lse.astype(jnp.bfloat16).astype(jnp.float32)
    rest = lse - high
    mid = rest.astype(jnp.bfloat16).astype(jnp.float32)
    low = rest - mid
    return jnp.where(lane < 16, high, jnp.where(lane < 32, mid, jnp.where(lane < 48, low, 0.0))).astype(jnp.bfloat16)


def decode_kernel(info, q_ref, k_ref, v_ref, o_ref):
    own_len = info[0]
    lane = lax.broadcasted_iota(jnp.int32, (GROUP * ROWS, SLOTS), 1)
    spot = lax.broadcasted_iota(jnp.int32, (ROWS, 128), 1) % 16
    lse = jnp.zeros((ROWS, 128), jnp.float32)
    for kv in range(KV):
        cols = pl.ds(kv * HEAD, HEAD)
        q = jnp.concatenate(
            [q_ref[:, pl.ds((kv * GROUP + g) * HEAD, HEAD)] for g in range(GROUP)], axis=0
        )
        scores = jnp.where(lane < own_len, qk(q, k_ref[:, cols]), NEG)
        top = jnp.max(scores, axis=1, keepdims=True)
        powers = jnp.exp2((scores - top) * EXP2_SCALE)
        total = jnp.sum(powers, axis=1, keepdims=True)
        weighted = pv(powers, v_ref[:, cols]) / total
        level = top * EXP2_SCALE + jnp.log2(total)
        for g in range(GROUP):
            rows = slice(g * ROWS, (g + 1) * ROWS)
            head = kv * GROUP + g
            o_ref[:, pl.ds(head * HEAD, HEAD)] = weighted[rows].astype(jnp.bfloat16)
            lse = jnp.where(spot == head, level[rows], lse)
    o_ref[:, pl.ds(WIDE, 128)] = pack_lse(lse)


def decode(info, rows, keys, values):
    return pl.pallas_call(
        decode_kernel,
        in_specs=[pl.BlockSpec(memory_space=pltpu.SMEM)] + [pl.BlockSpec(memory_space=pltpu.VMEM)] * 3,
        out_specs=pl.BlockSpec(memory_space=pltpu.VMEM),
        out_shape=jax.ShapeDtypeStruct((ROWS, MESSAGE), jnp.bfloat16),
        compiler_params=pltpu.CompilerParams(vmem_limit_bytes=32 << 20),
        cost_estimate=pl.CostEstimate(
            flops=4 * KV * GROUP * ROWS * SLOTS * HEAD, bytes_accessed=1 << 20, transcendentals=KV * GROUP * ROWS * SLOTS
        ),
        name="decode_part",
    )(info, rows, keys, values)


def merge_kernel(last, in_ref, o_ref):
    sources, rows, _ = in_ref.shape
    levels = []
    for s in range(sources):
        parts = in_ref[s, :, pl.ds(WIDE, 128)].astype(jnp.float32)
        levels.append(parts + pltpu.roll(parts, 112, 1) + pltpu.roll(parts, 96, 1))
    top = functools.reduce(jnp.maximum, levels)
    shares = [jnp.exp2(level - top) for level in levels]
    total = functools.reduce(jnp.add, shares)
    shares = [share / total for share in shares]
    copies = o_ref.shape[0]
    for head in range(KV * GROUP):
        cols = pl.ds(head * HEAD, HEAD)
        merged = jnp.zeros((rows, HEAD), jnp.float32)
        for s in range(sources):
            merged += shares[s][:, head : head + 1] * in_ref[s, :, cols].astype(jnp.float32)
        merged = merged.astype(jnp.bfloat16)
        for copy in range(copies):
            o_ref[copy, :, cols] = merged
    if not last:
        lane = lax.broadcasted_iota(jnp.int32, (rows, 128), 1)
        level = jnp.where(lane < 16, top + jnp.log2(total), 0.0)
        level = level + pltpu.roll(level, 16, 1) + pltpu.roll(level, 32, 1)
        packed = pack_lse(level)
        for copy in range(copies):
            o_ref[copy, :, pl.ds(WIDE, 128)] = packed


def merge(parts, copies, last):
    _, rows, _ = parts.shape
    return pl.pallas_call(
        functools.partial(merge_kernel, last),
        in_specs=[pl.BlockSpec(memory_space=pltpu.VMEM)],
        out_specs=pl.BlockSpec(memory_space=pltpu.VMEM),
        out_shape=jax.ShapeDtypeStruct((copies, rows, WIDE if last else MESSAGE), jnp.bfloat16),
        cost_estimate=pl.CostEstimate(flops=1 << 20, bytes_accessed=1 << 19, transcendentals=1 << 12),
        name="merge_parts",
    )(parts)


def fetch_anchor(keys, values, at):
    x, z, core = at
    perm = lambda block, pairs: lax.ppermute(block, "ctx", pairs)
    with jax.named_scope("anchor_core"):
        sent = perm(values, [(ctx_at(0, 0, 0), ctx_at(0, 0, 1))])
        held = jnp.where(core == 0, keys, sent)

    def across_x(core, zs):
        return [[(ctx_at(0, q, core), ctx_at(t, q, core)) for q in zs] for t in (1, 3, 2)]

    def across_z(core, xs, hops):
        return [[(ctx_at(q, s, core), ctx_at(q, t, core)) for q in xs for s, t in hop] for hop in hops]

    far = [[(0, 3)], [(0, 5)]]
    near = [[(0, 1), (3, 2), (5, 6)], [(0, 7), (3, 4)]]
    zs, xs = range(NZ), range(NX)
    stages = [
        (across_x(0, [0]), across_z(1, [0], far)),
        (across_z(0, xs, far), across_z(1, [0], near)),
        (across_z(0, xs, near), across_x(1, zs)),
    ]
    ctx = lax.axis_index("ctx")
    for number, (first, second) in enumerate(stages):
        with jax.named_scope(f"anchor_step{number}"):
            count = max(len(first), len(second))
            moves = [
                (first[i] if i < len(first) else []) + (second[i] if i < len(second) else []) for i in range(count)
            ]
            arrived = [perm(held, pairs) for pairs in moves]
            for block, pairs in zip(arrived, moves):
                hit = functools.reduce(jnp.logical_or, [ctx == target for _, target in pairs])
                held = jnp.where(hit, block, held)
    with jax.named_scope("anchor_swap"):
        other = perm(held, [(i, i ^ 1) for i in range(NX * NZ * NCORE)])
    return held, other


def body(queries, keys, values, block_lengths, decode_query_rows, out_weight):
    ctx = lax.axis_index("ctx")
    at = (ctx // (NZ * NCORE), (ctx // NCORE) % NZ, ctx % NCORE)
    own_len = block_lengths[ctx]
    anchor_len = jnp.where(ctx > 0, block_lengths[0], 0)
    info = jnp.stack([own_len, anchor_len, at[2]]).astype(jnp.int32)

    with jax.named_scope("rows_out"):
        spread = jnp.broadcast_to(decode_query_rows, (ROWS, WIDE))
        rows = lax.all_to_all(spread, "ctx", 0, 0, tiled=True)
    one, two = fetch_anchor(keys, values, at)

    message = decode(info, rows, keys, values)
    with jax.named_scope("parts_xc"):
        parts = lax.all_to_all(message, "ctx", 0, 0, axis_index_groups=XC_GROUPS, tiled=True)
    merged = merge(parts.reshape(8, 8, MESSAGE), NZ, False)
    with jax.named_scope("parts_z"):
        parts = lax.all_to_all(merged, "ctx", 0, 0, axis_index_groups=Z_GROUPS, tiled=True)
    attn = merge(parts, NX * NCORE, True)
    with jax.named_scope("attn_xc"):
        attn = lax.all_to_all(attn, "ctx", 0, 0, axis_index_groups=XC_GROUPS, tiled=True)
    projected = jnp.dot(attn.reshape(ROWS, WIDE), out_weight, preferred_element_type=jnp.float32)
    with jax.named_scope("tp_sum"):
        got = [lax.ppermute(projected, "tp", [(i, i ^ k) for i in range(NTP)]) for k in (1, 2, 3)]
        decode_out = ((projected + got[0]) + (got[1] + got[2])).astype(jnp.bfloat16)

    block_out = block_pass(0, info, queries, keys, values, one, two, None)
    block_out = block_pass(1, info, queries, keys, values, one, two, block_out)
    return block_out, decode_out


def solution(mesh):
    return jax.shard_map(
        body,
        mesh=mesh,
        in_specs=(
            P("ctx", "tp"),
            P("ctx", "tp"),
            P("ctx", "tp"),
            P(),
            P("ctx", "tp"),
            P("tp", "ctx"),
        ),
        out_specs=(P("ctx", "tp"), P(None, "ctx")),
        check_vma=False,
    )
```

time: 597 us -> 110 us (0.18)
  blocking collectives: 323 us -> 0 us
  waiting for transfers between devices: 203 us -> 21.4 us
  starting transfers between devices: 0.08 us -> 47.3 us
  Pallas kernels: 0 us -> 29.5 us
  matrix products: 29.9 us -> 1.17 us
  between operations: 14.2 us -> 1.86 us
  other arithmetic: 15.6 us -> 5.35 us
  local copies, waits for them, and re-layouts: 10.1 us -> 2.7 us
    psum x2 -> x0, waiting for transfers between devices: 203 us -> none  [the longest x1 167 us: broadcast(): return lax.psum(block, axis)]
    psum x2 -> x0, blocking collectives: 143 us -> none  [the longest x1 129 us: body(): lax.psum((dec_totals * factors, dec_weighted * factors[..., None]), 'ctx')]
    pmax x1 -> x0, blocking collectives: 126 us -> none  [body(): overall = lax.pmax(dec_top, 'ctx')]
    all_gather x1 -> x0, blocking collectives: 54.7 us -> none  [body(): decode_all = lax.all_gather(decode_query_rows, 'ctx', axis=0, tiled=True)]
    pallas_call x0 -> x5, Pallas kernels: none -> 29.5 us  [the longest x2 23.1 us: block_pass(): pl.pallas_call(block_kernel, grid_spec=pltpu.PrefetchScalarGridSpec(num_s...]
    dot_general x6 -> x1, matrix products: 29.9 us -> 1.17 us  [body(): jnp.dot(attn.reshape(ROWS, WIDE), out_weight, preferred_element_type=jnp....]
    ppermute x0 -> x13, starting transfers between devices: none -> 27.7 us  [the longest x10 23.9 us: fetch_anchor(): perm = lambda block, pairs: lax.ppermute(block, 'ctx', pairs)]
    all_to_all x0 -> x4, starting transfers between devices: none -> 19.6 us  [the longest x1 6.65 us: body(): lax.all_to_all(attn, 'ctx', 0, 0, axis_index_groups=XC_GROUPS, tiled=True)]
  transfers between devices with their start and end apart: 2 -> 17, of which waited for: 2 -> 4; matrix products, arithmetic and copies ran while one was open for 2% -> 7% of each run, Pallas kernels for 0% -> 27%
where the time goes in v1:
time: 110 us; the launch traced here: 109 us
  starting transfers between devices  47.3 us (43%)
  Pallas kernels  29.5 us (27%)
  waiting for transfers between devices  21.4 us (19%)
  other arithmetic  5.35 us (5%)
  local copies, waits for them, and re-layouts  2.7 us (2%)
  between operations  1.86 us (2%)
  matrix products  1.17 us (1%)
    ppermute x10, starting transfers between devices, fetch_anchor(): perm = lambda block, pairs: lax.ppermute(block, 'ctx', pairs)  23.9 us
    pallas_call x2, Pallas kernels, block_pass(): pl.pallas_call(block_kernel, grid_spec=pltpu.PrefetchScalarGridSpec(num_s...  23.1 us
    all_to_all x1, waiting for transfers between devices, body(): lax.all_to_all(merged, 'ctx', 0, 0, axis_index_groups=Z_GROUPS, tiled=True)  8.15 us
    all_to_all x1, starting transfers between devices, body(): lax.all_to_all(attn, 'ctx', 0, 0, axis_index_groups=XC_GROUPS, tiled=True)  6.65 us
    all_to_all x1, waiting for transfers between devices, body(): lax.all_to_all(message, 'ctx', 0, 0, axis_index_groups=XC_GROUPS, tiled=T...  4.89 us
    all_to_all x1, starting transfers between devices, body(): rows = lax.all_to_all(spread, 'ctx', 0, 0, tiled=True)  4.76 us
    ppermute x10, waiting for transfers between devices, fetch_anchor(): perm = lambda block, pairs: lax.ppermute(block, 'ctx', pairs)  4.46 us
    all_to_all x1, starting transfers between devices, body(): lax.all_to_all(message, 'ctx', 0, 0, axis_index_groups=XC_GROUPS, tiled=T...  4.14 us
  transfers between devices with their start and end apart: 17, of which 4 were waited for; matrix products, arithmetic and copies ran while one was open for 7% of the time, Pallas kernels for 27%

profile of v1, /device:TPU:1, one launch (start us, length us, event | category | flops | bytes accessed | tf_op | source)
XLA Modules:
  0.0 109.2 jit_solution(636208468263701799)
XLA Ops:
  0.6 0.0 copy-start
  0.6 1.4 %collective-permute-start = (bf16[512,256]{1,0:T(8,128)(2,1)}, bf16[512,256]{1,0:T(8,128)(2,1)S(1)}, u32[]{:S(2)}, u32[]{:S(2)}) collective-permute-start(bf16[512,256]{1,0:T(8,128)(2,1)} %v_ref.5), channel_id=1, source_target_pairs={{0,4},{1,5},{2,6},{3,7}} | collective-permute-start | bytes 786440 | tf_op jit(solution)/shard_map/anchor_core/ppermute | solution.py:187
  2.1 4.4 %collective-permute-done = bf16[512,256]{1,0:T(8,128)(2,1)S(1)} collective-permute-done((bf16[512,256]{1,0:T(8,128)(2,1)}, bf16[512,256]{1,0:T(8,128)(2,1)S(1)}, u32[]{:S(2)}, u32[]{:S(2)}) %collective-permute-start) | collective-permute-done | bytes 262176 | tf_op jit(solution)/shard_map/anchor_core/ppermute | solution.py:187
  6.6 0.7 collective-permute-start.1
  7.3 4.2 %collective-permute-start.2 = (bf16[512,256]{1,0:T(8,128)(2,1)S(1)}, bf16[512,256]{1,0:T(8,128)(2,1)S(1)}, u32[]{:S(2)}, u32[]{:S(2)}) collective-permute-start(bf16[512,256]{1,0:T(8,128)(2,1)S(1)} %broadcast_select_fusion), channel_id=1, source_target_pairs={{0,192},{4,44},{1,193},{5,45},{2,194},{6,46},{3,195},{7,47}} | collective-permute-start | bytes 786440 | tf_op jit(solution)/shard_map/anchor_step0/ppermute | solution.py:187
  11.5 1.3 %collective-permute-start.3 = (bf16[512,256]{1,0:T(8,128)(2,1)S(1)}, bf16[512,256]{1,0:T(8,128)(2,1)S(1)}, u32[]{:S(2)}, u32[]{:S(2)}) collective-permute-start(bf16[512,256]{1,0:T(8,128)(2,1)S(1)} %broadcast_select_fusion), channel_id=1, source_target_pairs={{0,64},{4,28},{1,65},{5,29},{2,66},{6,30},{3,67},{7,31}} | collective-permute-start | bytes 786440 | tf_op jit(solution)/shard_map/anchor_step0/ppermute | solution.py:187
  12.8 0.7 reduce
  13.5 0.3 broadcast_in_dim.2
  13.8 0.5 broadcast.6
  14.3 2.2 %reduce.1 = bf16[64,2048]{1,0:T(8,128)(2,1)S(1)} reduce(bf16[64,1,2048]{2,1,0:T(2,128)(2,1)S(1)} %broadcast_in_dim.2, bf16[]{:T(256)} %broadcast.6), dimensions={1}, to_apply=%broadcast_in_dim.2.reduce_sub_computation | reduce | bytes 524290 | tf_op jit(solution)/shard_map/rows_out/broadcast_in_dim | solution.py:230
  16.4 0.9 reshape.19
  17.3 4.8 %all-to-all-start = ((bf16[64,2,1024]{2,1,0:T(2,128)(2,1)}), bf16[64,2,1024]{2,1,0:T(2,128)(2,1)S(1)}, u32[]{:S(2)}, u32[]{:S(2)}) async-start(bf16[64,2,1024]{2,1,0:T(2,128)(2,1)} %reshape.19), calls=%async_computation | async-start | bytes 524288 | tf_op jit(solution)/shard_map/rows_out/all_to_all | solution.py:231
  22.1 0.0 copy-start.1
  22.1 0.0 copy-start.2
  22.1 0.0 collective-permute-done.1
  22.2 0.0 collective-permute-done.3
  22.2 0.1 select_select_fusion.2
  22.2 4.7 %collective-permute-start.4 = (bf16[512,256]{1,0:T(8,128)(2,1)S(1)}, bf16[512,256]{1,0:T(8,128)(2,1)S(1)}, u32[]{:S(2)}, u32[]{:S(2)}) collective-permute-start(bf16[512,256]{1,0:T(8,128)(2,1)S(1)} %select_select_fusion.2), channel_id=1, source_target_pairs={{0,40},{64,104},{128,168},{192,232},{4,60},{28,36},{1,41},{65,105}... | collective-permute-start | bytes 786440 | tf_op jit(solution)/shard_map/anchor_step1/ppermute | solution.py:187
  26.9 1.3 %collective-permute-start.5 = (bf16[512,256]{1,0:T(8,128)(2,1)S(1)}, bf16[512,256]{1,0:T(8,128)(2,1)S(1)}, u32[]{:S(2)}, u32[]{:S(2)}) collective-permute-start(bf16[512,256]{1,0:T(8,128)(2,1)S(1)} %select_select_fusion.2), channel_id=1, source_target_pairs={{0,24},{64,88},{128,152},{192,216},{4,12},{28,20},{44,52},{1,25},{... | collective-permute-start | bytes 786440 | tf_op jit(solution)/shard_map/anchor_step1/ppermute | solution.py:187
  28.2 0.6 fusion.2
  29.6 0.7 pad_add_fusion.info
  30.3 3.8 %all-to-all-done = bf16[64,2,1024]{2,1,0:T(2,128)(2,1)S(1)} async-done(((bf16[64,2,1024]{2,1,0:T(2,128)(2,1)}), bf16[64,2,1024]{2,1,0:T(2,128)(2,1)S(1)}, u32[]{:S(2)}, u32[]{:S(2)}) %all-to-all-start) | async-done | bytes 262176 | tf_op jit(solution)/shard_map/rows_out/all_to_all | solution.py:231
  34.1 0.2 reshape.20
  34.3 0.2 copy.11
  34.5 0.0 collective-permute-done.5
  34.6 5.1 %collective-permute-start.6 = (bf16[512,256]{1,0:T(8,128)(2,1)S(1)}, bf16[512,256]{1,0:T(8,128)(2,1)}, u32[]{:S(2)}, u32[]{:S(2)}) collective-permute-start(bf16[512,256]{1,0:T(8,128)(2,1)S(1)} %select_select_fusion.1), channel_id=1, source_target_pairs={{4,132},{12,140},{20,148},{28,156},{36,164},{44,172},{52,180},{60,... | collective-permute-start | bytes 786440 | tf_op jit(solution)/shard_map/anchor_step2/ppermute | solution.py:187
  39.7 2.0 %collective-permute-start.7 = (bf16[512,256]{1,0:T(8,128)(2,1)S(1)}, bf16[512,256]{1,0:T(8,128)(2,1)}, u32[]{:S(2)}, u32[]{:S(2)}) collective-permute-start(bf16[512,256]{1,0:T(8,128)(2,1)S(1)} %select_select_fusion.1), channel_id=1, source_target_pairs={{0,56},{24,32},{64,120},{88,96},{128,184},{152,160},{192,248},{216... | collective-permute-start | bytes 786440 | tf_op jit(solution)/shard_map/anchor_step2/ppermute | solution.py:187
  41.7 2.0 %collective-permute-start.8 = (bf16[512,256]{1,0:T(8,128)(2,1)S(1)}, bf16[512,256]{1,0:T(8,128)(2,1)}, u32[]{:S(2)}, u32[]{:S(2)}) collective-permute-start(bf16[512,256]{1,0:T(8,128)(2,1)S(1)} %select_select_fusion.1), channel_id=1, source_target_pairs={{0,8},{24,16},{40,48},{64,72},{88,80},{104,112},{128,136},{152,144... | collective-permute-start | bytes 786440 | tf_op jit(solution)/shard_map/anchor_step2/ppermute | solution.py:187
  43.7 2.4 %decode_part.1 = bf16[64,2176]{1,0:T(8,128)(2,1)} custom-call(s32[3]{0:T(128)S(1)} %pad_add_fusion.info, bf16[64,2048]{1,0:T(8,128)(2,1)S(1)} %bitcast.11, bf16[512,256]{1,0:T(8,128)(2,1)S(1)} %copy-done.1, bf16[512,256]{1,0:T(8,128)(2,1)S(1)} %copy-done.2), custom_call_target="tpu_custom_call" | custom-call | flops 268435456 | bytes 1048576 | tf_op jit(solution)/shard_map/decode_part/pallas_call | solution.py:132
  46.0 4.1 %all-to-all-start.1 = ((bf16[8,8,2176]{2,1,0:T(8,128)(2,1)}), bf16[8,8,2176]{2,1,0:T(8,128)(2,1)}, u32[]{:S(2)}, u32[]{:S(2)}) async-start(bf16[8,8,2176]{2,1,0:T(8,128)(2,1)} %bitcast.3), calls=%async_computation.1 | async-start | bytes 557056 | tf_op jit(solution)/shard_map/parts_xc/all_to_all | solution.py:236
  50.4 4.9 %all-to-all-done.1.in_ref = bf16[8,8,2176]{2,1,0:T(8,128)(2,1)} async-done(((bf16[8,8,2176]{2,1,0:T(8,128)(2,1)}), bf16[8,8,2176]{2,1,0:T(8,128)(2,1)}, u32[]{:S(2)}, u32[]{:S(2)}) %all-to-all-start.1) | async-done | bytes 278560 | tf_op jit(solution)/shard_map/parts_xc/all_to_all | solution.py:236
  55.3 2.0 %merge_parts.2 = bf16[8,8,2176]{2,1,0:T(8,128)(2,1)} custom-call(bf16[8,8,2176]{2,1,0:T(8,128)(2,1)} %all-to-all-done.1.in_ref), custom_call_target="tpu_custom_call" | custom-call | flops 1048576 | bytes 524288 | tf_op jit(solution)/shard_map/merge_parts/pallas_call | solution.py:175
  57.3 4.0 %all-to-all-start.2 = ((bf16[8,8,2176]{2,1,0:T(8,128)(2,1)}), bf16[8,8,2176]{2,1,0:T(8,128)(2,1)}, u32[]{:S(2)}, u32[]{:S(2)}) async-start(bf16[8,8,2176]{2,1,0:T(8,128)(2,1)} %merge_parts.2), calls=%async_computation.2 | async-start | bytes 557056 | tf_op jit(solution)/shard_map/parts_z/all_to_all | solution.py:239
  61.4 0.0 collective-permute-done.6
  61.4 0.0 collective-permute-done.7
  61.4 1.0 select_select_fusion.one_ref
  62.4 1.2 %collective-permute-start.9 = (bf16[512,256]{1,0:T(8,128)(2,1)S(1)}, bf16[512,256]{1,0:T(8,128)(2,1)}, u32[]{:S(2)}, u32[]{:S(2)}) collective-permute-start(bf16[512,256]{1,0:T(8,128)(2,1)S(1)} %select_select_fusion.one_ref), channel_id=1, source_target_pairs={{0,4},{4,0},{8,12},{12,8},{16,20},{20,16},{24,28},{28,24},{32,36},... | collective-permute-start | bytes 786440 | tf_op jit(solution)/shard_map/anchor_swap/ppermute | solution.py:187
  63.7 8.1 %all-to-all-done.2.in_ref = bf16[8,8,2176]{2,1,0:T(8,128)(2,1)} async-done(((bf16[8,8,2176]{2,1,0:T(8,128)(2,1)}), bf16[8,8,2176]{2,1,0:T(8,128)(2,1)}, u32[]{:S(2)}, u32[]{:S(2)}) %all-to-all-start.2) | async-done | bytes 278560 | tf_op jit(solution)/shard_map/parts_z/all_to_all | solution.py:239
  71.8 2.0 %merge_parts.3 = bf16[8,8,2048]{2,1,0:T(8,128)(2,1)} custom-call(bf16[8,8,2176]{2,1,0:T(8,128)(2,1)} %all-to-all-done.2.in_ref), custom_call_target="tpu_custom_call" | custom-call | flops 1048576 | bytes 524288 | tf_op jit(solution)/shard_map/merge_parts/pallas_call | solution.py:175
  73.8 6.7 %all-to-all-start.3 = ((bf16[8,8,2048]{2,1,0:T(8,128)(2,1)}), bf16[8,8,2048]{2,1,0:T(8,128)(2,1)}, u32[]{:S(2)}, u32[]{:S(2)}) async-start(bf16[8,8,2048]{2,1,0:T(8,128)(2,1)} %merge_parts.3), calls=%async_computation.3 | async-start | bytes 524288 | tf_op jit(solution)/shard_map/attn_xc/all_to_all | solution.py:242
  80.5 0.0 collective-permute-done.9.two_ref
  80.5 11.6 %block_pass.2.rest_0_ = bf16[512,2048]{1,0:T(8,128)(2,1)} custom-call(s32[3]{0:T(128)S(1)} %pad_add_fusion.info, bf16[512,2048]{1,0:T(8,128)(2,1)S(1)} %copy-done.3, bf16[512,256]{1,0:T(8,128)(2,1)S(1)} %copy-done.1, bf16[512,256]{1,0:T(8,128)(2,1)S(1)} %copy-done.2, bf16[512,256]{1,0:T(8,128)(2,1)S(1)} %select_select_fusion.one_ref, ...), custom_call_target="tpu_custom_call" | custom-call | flops 2147483648 | bytes 4194304 | tf_op jit(solution)/shard_map/block_pass/pallas_call | solution.py:80
  92.0 0.0 all-to-all-done.3
  92.0 1.2 %fusion = f32[64,128]{1,0:T(8,128)S(1)} fusion(bf16[2048,128]{1,0:T(8,128)(2,1)S(1)} %copy-done, bf16[8,8,2048]{2,1,0:T(8,128)(2,1)} %all-to-all-done.3), kind=kOutput, calls=%fused_computation.1 | convolution fusion | flops 33554432 | bytes 819200 | tf_op jit(solution)/shard_map/dot_general | solution.py:243
  93.2 3.0 %collective-permute-start.11 = (f32[64,128]{1,0:T(8,128)S(1)}, f32[64,128]{1,0:T(8,128)S(1)}, u32[]{:S(2)}, u32[]{:S(2)}) collective-permute-start(f32[64,128]{1,0:T(8,128)S(1)} %fusion), channel_id=1, source_target_pairs={{0,2},{1,3},{2,0},{3,1},{4,6},{5,7},{6,4},{7,5},{8,10},{9,11},{10,... | collective-permute-start | bytes 98312 | tf_op jit(solution)/shard_map/tp_sum/ppermute | solution.py:245
  96.2 0.8 collective-permute-start.12
  97.0 11.6 %block_pass.3 = bf16[512,2048]{1,0:T(8,128)(2,1)} custom-call(s32[3]{0:T(128)S(1)} %pad_add_fusion.info, bf16[512,2048]{1,0:T(8,128)(2,1)S(1)} %copy-done.3, bf16[512,256]{1,0:T(8,128)(2,1)S(1)} %copy-done.1, bf16[512,256]{1,0:T(8,128)(2,1)S(1)} %copy-done.2, bf16[512,256]{1,0:T(8,128)(2,1)S(1)} %select_select_fusion.one_ref, ...), custom_call_target="tpu_custom_call", output_to_operand_aliasing={{}: (6, {})} | custom-call | flops 2147483648 | bytes 4194304 | tf_op jit(solution)/shard_map/block_pass/pallas_call | solution.py:80
  108.6 0.6 add_convert_fusion
  (18 shorter events, 0.1 us)
Async XLA Ops:
  0.6 91.4 %copy-start = (bf16[2048,128]{1,0:T(8,128)(2,1)S(1)}, bf16[2048,128]{1,0:T(8,128)(2,1)}, u32[]{:S(2)}) copy-start(bf16[2048,128]{1,0:T(8,128)(2,1)} %param.11) | copy-start | bytes 1572868
  0.6 5.9 %collective-permute-start = (bf16[512,256]{1,0:T(8,128)(2,1)}, bf16[512,256]{1,0:T(8,128)(2,1)S(1)}, u32[]{:S(2)}, u32[]{:S(2)}) collective-permute-start(bf16[512,256]{1,0:T(8,128)(2,1)} %v_ref.5), channel_id=1, source_target_pairs={{0,4},{1,5},{2,6},{3,7}} | collective-permute-start | bytes 786440 | tf_op jit(solution)/shard_map/anchor_core/ppermute | solution.py:187
  2.1 26.1 %copy-start.5 = (s32[64]{0:T(128)S(1)}, s32[64]{0:T(128)}, u32[]{:S(2)}) copy-start(s32[64]{0:T(128)} %param.9) | copy-start | bytes 772
  6.6 15.6 %collective-permute-start.1 = (bf16[512,256]{1,0:T(8,128)(2,1)S(1)}, bf16[512,256]{1,0:T(8,128)(2,1)S(1)}, u32[]{:S(2)}, u32[]{:S(2)}) collective-permute-start(bf16[512,256]{1,0:T(8,128)(2,1)S(1)} %broadcast_select_fusion), channel_id=1, source_target_pairs={{0,128},{1,129},{2,130},{3,131}} | collective-permute-start | bytes 786440 | tf_op jit(solution)/shard_map/anchor_step0/ppermute | solution.py:187
  7.3 14.9 %collective-permute-start.2 = (bf16[512,256]{1,0:T(8,128)(2,1)S(1)}, bf16[512,256]{1,0:T(8,128)(2,1)S(1)}, u32[]{:S(2)}, u32[]{:S(2)}) collective-permute-start(bf16[512,256]{1,0:T(8,128)(2,1)S(1)} %broadcast_select_fusion), channel_id=1, source_target_pairs={{0,192},{4,44},{1,193},{5,45},{2,194},{6,46},{3,195},{7,47}} | collective-permute-start | bytes 786440 | tf_op jit(solution)/shard_map/anchor_step0/ppermute | solution.py:187
  11.5 10.7 %collective-permute-start.3 = (bf16[512,256]{1,0:T(8,128)(2,1)S(1)}, bf16[512,256]{1,0:T(8,128)(2,1)S(1)}, u32[]{:S(2)}, u32[]{:S(2)}) collective-permute-start(bf16[512,256]{1,0:T(8,128)(2,1)S(1)} %broadcast_select_fusion), channel_id=1, source_target_pairs={{0,64},{4,28},{1,65},{5,29},{2,66},{6,30},{3,67},{7,31}} | collective-permute-start | bytes 786440 | tf_op jit(solution)/shard_map/anchor_step0/ppermute | solution.py:187
  17.3 16.8 %all-to-all-start = ((bf16[64,2,1024]{2,1,0:T(2,128)(2,1)}), bf16[64,2,1024]{2,1,0:T(2,128)(2,1)S(1)}, u32[]{:S(2)}, u32[]{:S(2)}) async-start(bf16[64,2,1024]{2,1,0:T(2,128)(2,1)} %reshape.19), calls=%async_computation | async-start | bytes 524288 | tf_op jit(solution)/shard_map/rows_out/all_to_all | solution.py:231
  22.1 21.6 %copy-start.1 = (bf16[512,256]{1,0:T(8,128)(2,1)S(1)}, bf16[512,256]{1,0:T(8,128)(2,1)}, u32[]{:S(2)}) copy-start(bf16[512,256]{1,0:T(8,128)(2,1)} %k_ref.5) | copy-start | bytes 786436
  22.1 21.6 %copy-start.2 = (bf16[512,256]{1,0:T(8,128)(2,1)S(1)}, bf16[512,256]{1,0:T(8,128)(2,1)}, u32[]{:S(2)}) copy-start(bf16[512,256]{1,0:T(8,128)(2,1)} %v_ref.5) | copy-start | bytes 786436
  22.2 12.3 %collective-permute-start.4 = (bf16[512,256]{1,0:T(8,128)(2,1)S(1)}, bf16[512,256]{1,0:T(8,128)(2,1)S(1)}, u32[]{:S(2)}, u32[]{:S(2)}) collective-permute-start(bf16[512,256]{1,0:T(8,128)(2,1)S(1)} %select_select_fusion.2), channel_id=1, source_target_pairs={{0,40},{64,104},{128,168},{192,232},{4,60},{28,36},{1,41},{65,105}... | collective-permute-start | bytes 786440 | tf_op jit(solution)/shard_map/anchor_step1/ppermute | solution.py:187
  26.9 7.6 %collective-permute-start.5 = (bf16[512,256]{1,0:T(8,128)(2,1)S(1)}, bf16[512,256]{1,0:T(8,128)(2,1)S(1)}, u32[]{:S(2)}, u32[]{:S(2)}) collective-permute-start(bf16[512,256]{1,0:T(8,128)(2,1)S(1)} %select_select_fusion.2), channel_id=1, source_target_pairs={{0,24},{64,88},{128,152},{192,216},{4,12},{28,20},{44,52},{1,25},{... | collective-permute-start | bytes 786440 | tf_op jit(solution)/shard_map/anchor_step1/ppermute | solution.py:187
  34.6 26.8 %copy-start.4 = (bf16[512,256]{1,0:T(8,128)(2,1)}, bf16[512,256]{1,0:T(8,128)(2,1)S(1)}, u32[]{:S(2)}) copy-start(bf16[512,256]{1,0:T(8,128)(2,1)S(1)} %select_select_fusion.1) | copy-start | bytes 786436
  34.6 26.8 %collective-permute-start.6 = (bf16[512,256]{1,0:T(8,128)(2,1)S(1)}, bf16[512,256]{1,0:T(8,128)(2,1)}, u32[]{:S(2)}, u32[]{:S(2)}) collective-permute-start(bf16[512,256]{1,0:T(8,128)(2,1)S(1)} %select_select_fusion.1), channel_id=1, source_target_pairs={{4,132},{12,140},{20,148},{28,156},{36,164},{44,172},{52,180},{60,... | collective-permute-start | bytes 786440 | tf_op jit(solution)/shard_map/anchor_step2/ppermute | solution.py:187
  39.7 21.7 %collective-permute-start.7 = (bf16[512,256]{1,0:T(8,128)(2,1)S(1)}, bf16[512,256]{1,0:T(8,128)(2,1)}, u32[]{:S(2)}, u32[]{:S(2)}) collective-permute-start(bf16[512,256]{1,0:T(8,128)(2,1)S(1)} %select_select_fusion.1), channel_id=1, source_target_pairs={{0,56},{24,32},{64,120},{88,96},{128,184},{152,160},{192,248},{216... | collective-permute-start | bytes 786440 | tf_op jit(solution)/shard_map/anchor_step2/ppermute | solution.py:187
  41.7 19.7 %collective-permute-start.8 = (bf16[512,256]{1,0:T(8,128)(2,1)S(1)}, bf16[512,256]{1,0:T(8,128)(2,1)}, u32[]{:S(2)}, u32[]{:S(2)}) collective-permute-start(bf16[512,256]{1,0:T(8,128)(2,1)S(1)} %select_select_fusion.1), channel_id=1, source_target_pairs={{0,8},{24,16},{40,48},{64,72},{88,80},{104,112},{128,136},{152,144... | collective-permute-start | bytes 786440 | tf_op jit(solution)/shard_map/anchor_step2/ppermute | solution.py:187
  46.0 34.4 %copy-start.3 = (bf16[512,2048]{1,0:T(8,128)(2,1)S(1)}, bf16[512,2048]{1,0:T(8,128)(2,1)}, u32[]{:S(2)}) copy-start(bf16[512,2048]{1,0:T(8,128)(2,1)} %q_ref.3) | copy-start | bytes 6291460
  46.0 9.3 %all-to-all-start.1 = ((bf16[8,8,2176]{2,1,0:T(8,128)(2,1)}), bf16[8,8,2176]{2,1,0:T(8,128)(2,1)}, u32[]{:S(2)}, u32[]{:S(2)}) async-start(bf16[8,8,2176]{2,1,0:T(8,128)(2,1)} %bitcast.3), calls=%async_computation.1 | async-start | bytes 557056 | tf_op jit(solution)/shard_map/parts_xc/all_to_all | solution.py:236
  57.3 14.5 %all-to-all-start.2 = ((bf16[8,8,2176]{2,1,0:T(8,128)(2,1)}), bf16[8,8,2176]{2,1,0:T(8,128)(2,1)}, u32[]{:S(2)}, u32[]{:S(2)}) async-start(bf16[8,8,2176]{2,1,0:T(8,128)(2,1)} %merge_parts.2), calls=%async_computation.2 | async-start | bytes 557056 | tf_op jit(solution)/shard_map/parts_z/all_to_all | solution.py:239
  62.4 18.0 %collective-permute-start.9 = (bf16[512,256]{1,0:T(8,128)(2,1)S(1)}, bf16[512,256]{1,0:T(8,128)(2,1)}, u32[]{:S(2)}, u32[]{:S(2)}) collective-permute-start(bf16[512,256]{1,0:T(8,128)(2,1)S(1)} %select_select_fusion.one_ref), channel_id=1, source_target_pairs={{0,4},{4,0},{8,12},{12,8},{16,20},{20,16},{24,28},{28,24},{32,36},... | collective-permute-start | bytes 786440 | tf_op jit(solution)/shard_map/anchor_swap/ppermute | solution.py:187
  73.8 18.2 %all-to-all-start.3 = ((bf16[8,8,2048]{2,1,0:T(8,128)(2,1)}), bf16[8,8,2048]{2,1,0:T(8,128)(2,1)}, u32[]{:S(2)}, u32[]{:S(2)}) async-start(bf16[8,8,2048]{2,1,0:T(8,128)(2,1)} %merge_parts.3), calls=%async_computation.3 | async-start | bytes 524288 | tf_op jit(solution)/shard_map/attn_xc/all_to_all | solution.py:242
  93.2 15.4 %collective-permute-start.11 = (f32[64,128]{1,0:T(8,128)S(1)}, f32[64,128]{1,0:T(8,128)S(1)}, u32[]{:S(2)}, u32[]{:S(2)}) collective-permute-start(f32[64,128]{1,0:T(8,128)S(1)} %fusion), channel_id=1, source_target_pairs={{0,2},{1,3},{2,0},{3,1},{4,6},{5,7},{6,4},{7,5},{8,10},{9,11},{10,... | collective-permute-start | bytes 98312 | tf_op jit(solution)/shard_map/tp_sum/ppermute | solution.py:245
  96.2 12.4 %collective-permute-start.12 = (f32[64,128]{1,0:T(8,128)S(1)}, f32[64,128]{1,0:T(8,128)S(1)}, u32[]{:S(2)}, u32[]{:S(2)}) collective-permute-start(f32[64,128]{1,0:T(8,128)S(1)} %fusion), channel_id=1, source_target_pairs={{0,3},{1,2},{2,1},{3,0},{4,7},{5,6},{6,5},{7,4},{8,11},{9,10},{10,... | collective-permute-start | bytes 98312 | tf_op jit(solution)/shard_map/tp_sum/ppermute | solution.py:245
  97.0 11.6 %collective-permute-start.10 = (f32[64,128]{1,0:T(8,128)S(1)}, f32[64,128]{1,0:T(8,128)S(1)}, u32[]{:S(2)}, u32[]{:S(2)}) collective-permute-start(f32[64,128]{1,0:T(8,128)S(1)} %fusion), channel_id=1, source_target_pairs={{0,1},{1,0},{2,3},{3,2},{4,5},{5,4},{6,7},{7,6},{8,9},{9,8},{10,11... | collective-permute-start | bytes 98312 | tf_op jit(solution)/shard_map/tp_sum/ppermute | solution.py:245

commit v2 on v1

v2 whole, which is shorter than its diff:
```python
import functools
import math

import jax
import jax.numpy as jnp
from jax import lax
from jax.experimental import pallas as pl
from jax.experimental.pallas import tpu as pltpu
from jax.sharding import PartitionSpec as P

HEAD = 128
GROUP = 8
KV = 2
SLOTS = 512
HALF = 256
ROWS = 64
NX, NZ, NCORE, NTP = 4, 8, 2, 4
WIDE = KV * GROUP * HEAD
MESSAGE = WIDE + 128
EXP2_SCALE = HEAD**-0.5 * math.log2(math.e)
NEG = -1e30
NT = (((1,), (1,)), ((), ()))


def ctx_at(x, z, core):
    return (x * NZ + z) * NCORE + core


NEAR, FAR = 16, 4
NEAR_GROUPS = [
    [ctx_at(x, 2 * far + z, c) for x in range(NX) for z in range(2) for c in range(NCORE)] for far in range(FAR)
]
FAR_GROUPS = [
    [ctx_at(x, 2 * far + z, c) for far in range(FAR)] for x in range(NX) for z in range(2) for c in range(NCORE)
]
EACH = ROWS // NEAR


def qk(q, k):
    return lax.dot_general(q, k, NT, preferred_element_type=jnp.float32)


def pv(p, v):
    return jnp.dot(p.astype(jnp.bfloat16), v, preferred_element_type=jnp.float32)


def scaled(keys):
    wide = keys.astype(jnp.float32) * EXP2_SCALE
    high = wide.astype(jnp.bfloat16)
    return jnp.concatenate([high, (wide - high.astype(jnp.float32)).astype(jnp.bfloat16)], axis=1)


def with_ones(values):
    return jnp.concatenate([values, jnp.ones_like(values)], axis=1)


def max_of(pieces):
    tiles = [piece[:, i : i + HEAD] for piece in pieces for i in range(0, piece.shape[1], HEAD)]
    return jnp.max(functools.reduce(jnp.maximum, tiles), axis=1, keepdims=True)


def block_kernel(heads, lens, q_ref, k_ref, v_ref, one_ref, two_ref, *rest):
    o_ref = rest[-1]
    ctx = lax.axis_index("ctx")
    own_len, anchor_len = lens[ctx], lens[0]
    row = lax.broadcasted_iota(jnp.int32, (HALF, HALF), 0)
    lane = lax.broadcasted_iota(jnp.int32, (HALF, HALF), 1)

    def run(anchored):
        own_keys, own_values = scaled(k_ref[...]), with_ones(v_ref[...])
        if anchored:
            swap = lax.rem(ctx, NCORE) > 0
            one, two = one_ref[...], two_ref[...]
            anchor_keys = scaled(jnp.where(swap, two, one))
            anchor_values = with_ones(jnp.where(swap, one, two))

        def score(h, part):
            q = q_ref[pl.ds(part * HALF, HALF), h * HEAD : (h + 1) * HEAD]
            q = jnp.concatenate([q, q], axis=1)
            return qk(q, own_keys[: HALF * (part + 1)]), qk(q, anchor_keys) if anchored else None

        def share(part, own, anchor):
            pieces = [own[:, :HALF]] if part else []
            pieces.append(jnp.where(lane <= row, own[:, part * HALF :], NEG))
            if anchored:
                pieces += [anchor[:, :HALF], jnp.where(lane + HALF < anchor_len, anchor[:, HALF:], NEG)]
            top = max_of(pieces)
            shares = [jnp.exp2(piece - top).astype(jnp.bfloat16) for piece in pieces]
            cut = part + 1
            return jnp.concatenate(shares[:cut], axis=1), jnp.concatenate(shares[cut:], axis=1) if anchored else None

        def finish(h, part, own, anchor):
            both = jnp.dot(own, own_values[: HALF * (part + 1)], preferred_element_type=jnp.float32)
            if anchored:
                both += jnp.dot(anchor, anchor_values, preferred_element_type=jnp.float32)
            live = lax.broadcasted_iota(jnp.int32, (HALF, HEAD), 0) + part * HALF < own_len
            out = jnp.where(live, both[:, :HEAD] * (1.0 / both[:, HEAD:]), 0.0)
            o_ref[pl.ds(part * HALF, HALF), h * HEAD : (h + 1) * HEAD] = out.astype(o_ref.dtype)

        items = [(h, part) for h in range(heads) for part in range(2)]
        scores, shares = score(*items[0]), None
        for i, (h, part) in enumerate(items):
            later = score(*items[i + 1]) if i + 1 < len(items) else None
            now = share(part, *scores)
            if shares is not None:
                finish(*items[i - 1], *shares)
            scores, shares = later, now
        finish(*items[-1], *shares)

    pl.when(ctx > 0)(lambda: run(True))
    pl.when(ctx == 0)(lambda: run(False))


def block_pass(first, count, step, lens, queries, keys, values, one, two, out):
    head = lambda g, lens: (0, first // step + g)
    shared = lambda g, lens: (0, (first + g * step) // GROUP)
    specs = [pl.BlockSpec((SLOTS, step * HEAD), head)] + [pl.BlockSpec((SLOTS, HEAD), shared)] * 4
    operands = [queries, keys, values, one, two]
    aliases = {}
    if out is not None:
        specs.append(pl.BlockSpec(memory_space=pl.ANY))
        operands.append(out)
        aliases = {6: 0}
    return pl.pallas_call(
        functools.partial(block_kernel, step),
        grid_spec=pltpu.PrefetchScalarGridSpec(
            num_scalar_prefetch=1,
            grid=(count // step,),
            in_specs=specs,
            out_specs=pl.BlockSpec((SLOTS, step * HEAD), head),
        ),
        out_shape=jax.ShapeDtypeStruct(queries.shape, jnp.bfloat16),
        input_output_aliases=aliases,
        compiler_params=pltpu.CompilerParams(vmem_limit_bytes=56 << 20),
        cost_estimate=pl.CostEstimate(
            flops=count * SLOTS * SLOTS * HEAD * 8, bytes_accessed=4 << 20, transcendentals=count * SLOTS * 1024
        ),
        name="block_pass",
    )(lens, *operands)


def pack_lse(lse):
    lane = lax.broadcasted_iota(jnp.int32, lse.shape, 1)
    high = lse.astype(jnp.bfloat16).astype(jnp.float32)
    rest = lse - high
    mid = rest.astype(jnp.bfloat16).astype(jnp.float32)
    low = rest - mid
    return jnp.where(lane < 16, high, jnp.where(lane < 32, mid, jnp.where(lane < 48, low, 0.0))).astype(jnp.bfloat16)


def spread_kernel(row_ref, o_ref):
    row = row_ref[...].astype(jnp.float32)
    heads = jnp.concatenate([row[:, h * HEAD : (h + 1) * HEAD] for h in range(KV * GROUP)], axis=0)
    o_ref[...] = jnp.broadcast_to(heads.astype(jnp.bfloat16)[None], o_ref.shape)


def spread(row):
    return pl.pallas_call(
        spread_kernel,
        in_specs=[pl.BlockSpec(memory_space=pltpu.VMEM)],
        out_specs=pl.BlockSpec(memory_space=pltpu.VMEM),
        out_shape=jax.ShapeDtypeStruct((ROWS, KV * GROUP, HEAD), jnp.bfloat16),
        compiler_params=pltpu.CompilerParams(vmem_limit_bytes=8 << 20),
        cost_estimate=pl.CostEstimate(flops=1 << 16, bytes_accessed=1 << 18, transcendentals=0),
        name="spread_rows",
    )(row)


def decode_kernel(lens, q_ref, k_ref, v_ref, o_ref):
    own_len = lens[lax.axis_index("ctx")]
    lane = lax.broadcasted_iota(jnp.int32, (ROWS * GROUP, HALF), 1)
    spot = lax.broadcasted_iota(jnp.int32, (ROWS, 128), 1) % 16
    lse = jnp.zeros((ROWS, 128), jnp.float32)

    def put(cols, block):
        for n in range(NEAR):
            o_ref[n, :, cols] = block[n * EACH : (n + 1) * EACH]

    rows = q_ref[...].astype(jnp.float32)
    for kv in range(KV):
        cols = pl.ds(kv * HEAD, HEAD)
        q = rows[:, kv * GROUP : (kv + 1) * GROUP].reshape(ROWS * GROUP, HEAD).astype(jnp.bfloat16)
        scores = qk(q, k_ref[:, cols])
        near, far = scores[:, :HALF], jnp.where(lane + HALF < own_len, scores[:, HALF:], NEG)
        top = jnp.max(jnp.maximum(near, far), axis=1, keepdims=True)
        near, far = jnp.exp2((near - top) * EXP2_SCALE), jnp.exp2((far - top) * EXP2_SCALE)
        total = jnp.sum(near + far, axis=1, keepdims=True)
        weighted = pv(jnp.concatenate([near, far], axis=1), v_ref[:, cols]) * (1.0 / total)
        weighted = weighted.reshape(ROWS, GROUP, HEAD)
        level = jnp.broadcast_to(top * EXP2_SCALE + jnp.log2(total), (ROWS * GROUP, HEAD)).reshape(ROWS, GROUP, HEAD)
        for g in range(GROUP):
            head = kv * GROUP + g
            put(pl.ds(head * HEAD, HEAD), weighted[:, g].astype(jnp.bfloat16))
            lse = jnp.where(spot == head, level[:, g], lse)
    put(pl.ds(WIDE, 128), pack_lse(lse))


def decode(lens, rows, keys, values):
    return pl.pallas_call(
        decode_kernel,
        in_specs=[pl.BlockSpec(memory_space=pltpu.SMEM)] + [pl.BlockSpec(memory_space=pltpu.VMEM)] * 3,
        out_specs=pl.BlockSpec(memory_space=pltpu.VMEM),
        out_shape=jax.ShapeDtypeStruct((NEAR, EACH, MESSAGE), jnp.bfloat16),
        compiler_params=pltpu.CompilerParams(vmem_limit_bytes=32 << 20),
        cost_estimate=pl.CostEstimate(
            flops=4 * KV * GROUP * ROWS * SLOTS * HEAD, bytes_accessed=1 << 20, transcendentals=KV * GROUP * ROWS * SLOTS
        ),
        name="decode_part",
    )(lens, rows, keys, values)


def merge_kernel(last, in_ref, o_ref):
    tiles = in_ref.shape[0] // 2
    tile = lambda t, cols: jnp.concatenate([in_ref[2 * t + i, :, cols].astype(jnp.float32) for i in range(2)], axis=0)

    def across(op, parts):
        half = functools.reduce(op, parts)
        return op(half, pltpu.roll(half, EACH, 0))

    levels = []
    for t in range(tiles):
        parts = tile(t, pl.ds(WIDE, 128))
        levels.append(parts + pltpu.roll(parts, 112, 1) + pltpu.roll(parts, 96, 1))
    top = across(jnp.maximum, levels)
    shares = [jnp.exp2(level - top) for level in levels]
    total = across(jnp.add, shares)
    scale = 1.0 / total
    shares = [share * scale for share in shares]
    for head in range(KV * GROUP):
        cols = pl.ds(head * HEAD, HEAD)
        merged = across(jnp.add, [shares[t][:, head : head + 1] * tile(t, cols) for t in range(tiles)])
        o_ref[:, :, cols] = jnp.broadcast_to(merged[None, :EACH].astype(jnp.bfloat16), (o_ref.shape[0], EACH, HEAD))
    if not last:
        lane = lax.broadcasted_iota(jnp.int32, (2 * EACH, 128), 1)
        level = jnp.where(lane < 16, top + jnp.log2(total), 0.0)
        level = level + pltpu.roll(level, 16, 1) + pltpu.roll(level, 32, 1)
        o_ref[:, :, pl.ds(WIDE, 128)] = jnp.broadcast_to(pack_lse(level)[None, :EACH], (o_ref.shape[0], EACH, 128))


def merge(parts, copies, last):
    return pl.pallas_call(
        functools.partial(merge_kernel, last),
        in_specs=[pl.BlockSpec(memory_space=pltpu.VMEM)],
        out_specs=pl.BlockSpec(memory_space=pltpu.VMEM),
        out_shape=jax.ShapeDtypeStruct((copies, EACH, WIDE if last else MESSAGE), jnp.bfloat16),
        compiler_params=pltpu.CompilerParams(vmem_limit_bytes=8 << 20),
        cost_estimate=pl.CostEstimate(flops=1 << 20, bytes_accessed=1 << 19, transcendentals=1 << 12),
        name="merge_parts",
    )(parts)


def anchor_moves():
    near = [(0, 0), (1, 0), (0, 4), (1, 4)]
    keys_2 = [
        [((x, 0), (x + dx, dz)) for x in (0, 2)] for dx, dz in near[1:]
    ]
    values_2 = [
        [((0, z), (dx, z + dz)) for z in (0, 4)] for dx, dz in ((0, 2), (2, 0), (2, 2))
    ]
    keys_3 = [
        [((x, z), (x, (z + dz) % NZ)) for x in range(NX) for z in (0, 4)] for dz in (1, -1, 2)
    ]
    values_3 = [
        [((x, z), (x + dx, z + dz)) for x in (0, 2) for z in (0, 2, 4, 6)] for dx, dz in ((1, 0), (0, 1), (1, 1))
    ]

    def join(keys, values):
        return [
            [(ctx_at(*s, core), ctx_at(*t, core)) for core, pairs in enumerate(both) for s, t in pairs]
            for both in zip(keys, values)
        ]

    return join(keys_2, values_2), join(keys_3, values_3)


def fetch_anchor(keys, values, pins, later_pins):
    ctx = lax.axis_index("ctx")
    perm = lambda block, pairs: lax.ppermute(block, "ctx", pairs)

    def place(held, arrived, moves):
        for block, pairs in zip(arrived, moves):
            hit = functools.reduce(jnp.logical_or, [ctx == target for _, target in pairs])
            held = jnp.where(hit, block, held)
        return held

    with jax.named_scope("anchor_step1"):
        root = ctx_at(0, 0, 0)
        moves = [[(root, ctx_at(2, 0, 0))], [(root, ctx_at(0, 0, 1))], [(root, ctx_at(0, 4, 1))]]
        held = place(keys, [perm(block, pairs) for block, pairs in zip((keys, values, values), moves)], moves)
    for number, moves in enumerate(anchor_moves()):
        with jax.named_scope(f"anchor_step{number + 2}"):
            held, _ = lax.optimization_barrier((held, pins[number]))
            arrived = [perm(held, pairs) for pairs in moves]
            held, _ = lax.optimization_barrier((held, later_pins[number]))
            held = place(held, arrived, moves)
    with jax.named_scope("anchor_swap"):
        other = perm(held, [(i, i ^ 1) for i in range(NX * NZ * NCORE)])
    return held, other


def body(queries, keys, values, block_lengths, decode_query_rows, out_weight):
    with jax.named_scope("rows_out"):
        copies, keys, values = lax.optimization_barrier((spread(decode_query_rows), keys, values))
        rows = lax.all_to_all(copies, "ctx", 0, 0, tiled=True)
    message = decode(block_lengths, rows, keys, values)
    with jax.named_scope("parts_near"):
        parts = lax.all_to_all(message, "ctx", 0, 0, axis_index_groups=NEAR_GROUPS, tiled=True)
    merged = merge(parts, FAR, False)
    one, two = fetch_anchor(keys, values, (keys, message), (keys, keys))
    with jax.named_scope("parts_far"):
        parts = lax.all_to_all(merged, "ctx", 0, 0, axis_index_groups=FAR_GROUPS, tiled=True)
    attn = merge(parts, NEAR, True)
    with jax.named_scope("attn_near"):
        attn = lax.all_to_all(attn, "ctx", 0, 0, axis_index_groups=NEAR_GROUPS, tiled=True)
    projected = jnp.dot(attn.reshape(ROWS, WIDE), out_weight, preferred_element_type=jnp.float32)
    with jax.named_scope("tp_sum"):
        got = [lax.ppermute(projected, "tp", [(i, i ^ k) for i in range(NTP)]) for k in (1, 2, 3)]
        decode_out = ((projected + got[0]) + (got[1] + got[2])).astype(jnp.bfloat16)

    block_out = block_pass(0, 8, 8, block_lengths, queries, keys, values, one, two, None)
    block_out = block_pass(8, 8, 8, block_lengths, queries, keys, values, one, two, block_out)
    return block_out, decode_out


def solution(mesh):
    return jax.shard_map(
        body,
        mesh=mesh,
        in_specs=(
            P("ctx", "tp"),
            P("ctx", "tp"),
            P("ctx", "tp"),
            P(),
            P("ctx", "tp"),
            P("tp", "ctx"),
        ),
        out_specs=(P("ctx", "tp"), P(None, "ctx")),
        check_vma=False,
    )
```

time: 110 us -> 86 us (0.78)
  Pallas kernels: 29.5 us -> 20.5 us
  waiting for transfers between devices: 21.4 us -> 12.5 us
  other arithmetic: 5.35 us -> 1.76 us
  local copies, waits for them, and re-layouts: 2.7 us -> 1.57 us
    all_to_all x4, starting transfers between devices: 19.6 us -> 27.3 us  [the longest x1 13.5 us: body(): rows = lax.all_to_all(copies, 'ctx', 0, 0, tiled=True)]
    pallas_call x2 -> x3, Pallas kernels: 23.1 us -> 15.7 us  [the longest x2 15 us: block_pass(): pl.pallas_call(functools.partial(block_kernel, step), grid_spec=pltpu.Pre...]
    ppermute x10, starting transfers between devices: 23.9 us -> 16.9 us  [fetch_anchor(): perm = lambda block, pairs: lax.ppermute(block, 'ctx', pairs)]
    all_to_all x4, waiting for transfers between devices: 16.9 us -> 11 us  [the longest x1 6.85 us: body(): lax.all_to_all(merged, 'ctx', 0, 0, axis_index_groups=FAR_GROUPS, tiled=T...]
    ppermute x10, waiting for transfers between devices: 4.46 us -> 1.45 us  [fetch_anchor(): perm = lambda block, pairs: lax.ppermute(block, 'ctx', pairs)]
    broadcast_in_dim x1 -> x0, other arithmetic: 2.15 us -> none  [body(): spread = jnp.broadcast_to(decode_query_rows, (ROWS, WIDE))]
    pallas_call x2, Pallas kernels: 3.99 us -> 1.96 us  [merge(): pl.pallas_call(functools.partial(merge_kernel, last), in_specs=[pl.BlockS...]
  transfers between devices with their start and end apart: 17 -> 17, of which waited for: 4 -> 4; matrix products, arithmetic and copies ran while one was open for 7% -> 1% of each run, Pallas kernels for 27% -> 23%
where the time goes in v2:
time: 86 us; the launch traced here: 85.3 us
  starting transfers between devices  47.7 us (55%)
  Pallas kernels  20.5 us (24%)
  waiting for transfers between devices  12.5 us (15%)
  other arithmetic  1.76 us (2%)
  local copies, waits for them, and re-layouts  1.57 us (2%)
  between operations  1.14 us (1%)
    ppermute x10, starting transfers between devices, fetch_anchor(): perm = lambda block, pairs: lax.ppermute(block, 'ctx', pairs)  16.9 us
    pallas_call x2, Pallas kernels, block_pass(): pl.pallas_call(functools.partial(block_kernel, step), grid_spec=pltpu.Pre...  15 us
    all_to_all x1, starting transfers between devices, body(): rows = lax.all_to_all(copies, 'ctx', 0, 0, tiled=True)  13.5 us
    all_to_all x1, waiting for transfers between devices, body(): lax.all_to_all(merged, 'ctx', 0, 0, axis_index_groups=FAR_GROUPS, tiled=T...  6.85 us
    all_to_all x1, starting transfers between devices, body(): lax.all_to_all(attn, 'ctx', 0, 0, axis_index_groups=NEAR_GROUPS, tiled=True)  5.69 us
    all_to_all x1, starting transfers between devices, body(): lax.all_to_all(message, 'ctx', 0, 0, axis_index_groups=NEAR_GROUPS, tiled...  4.83 us
    ppermute x3, starting transfers between devices, body(): lax.ppermute(projected, 'tp', [(i, i ^ k) for i in range(NTP)])  3.5 us
    all_to_all x1, starting transfers between devices, body(): lax.all_to_all(merged, 'ctx', 0, 0, axis_index_groups=FAR_GROUPS, tiled=T...  3.29 us
  transfers between devices with their start and end apart: 17, of which 4 were waited for; matrix products, arithmetic and copies ran while one was open for 1% of the time, Pallas kernels for 23%

profile of v2, /device:TPU:1, one launch (start us, length us, event | category | flops | bytes accessed | tf_op | source)
XLA Modules:
  0.0 85.3 jit_solution(10376898146104144128)
XLA Ops:
  0.6 0.0 copy-start
  0.6 0.0 copy-start.2
  0.7 0.0 copy-start.1
  0.7 0.8 copy-done.3
  1.5 0.7 spread_rows.1
  2.2 1.3 %collective-permute-start.1 = (bf16[512,256]{1,0:T(8,128)(2,1)}, bf16[512,256]{1,0:T(8,128)(2,1)S(1)}, u32[]{:S(2)}, u32[]{:S(2)}) collective-permute-start(bf16[512,256]{1,0:T(8,128)(2,1)} %v_ref.2), channel_id=1, source_target_pairs={{0,4},{1,5},{2,6},{3,7}} | collective-permute-start | bytes 786440 | tf_op jit(solution)/shard_map/anchor_step1/ppermute | solution.py:278
  3.5 0.7 collective-permute-start
  4.2 0.7 collective-permute-start.2
  4.8 13.5 %all-to-all-start = ((bf16[64,16,128]{2,1,0:T(8,128)(2,1)}), bf16[64,16,128]{2,1,0:T(8,128)(2,1)S(1)}, u32[]{:S(2)}, u32[]{:S(2)}) async-start(bf16[64,16,128]{2,1,0:T(8,128)(2,1)} %spread_rows.1), calls=%async_computation | async-start | bytes 524288 | tf_op jit(solution)/shard_map/rows_out/all_to_all | solution.py:304
  18.3 0.0 collective-permute-done.1
  18.3 0.0 collective-permute-done
  18.3 0.0 collective-permute-done.2
  18.4 1.0 %select_select_fusion.2 = bf16[512,256]{1,0:T(8,128)(2,1)S(1)} fusion(bf16[512,256]{1,0:T(8,128)(2,1)S(1)} %collective-permute-done, bf16[512,256]{1,0:T(8,128)(2,1)S(1)} %collective-permute-done.1, bf16[512,256]{1,0:T(8,128)(2,1)S(1)} %collective-permute-done.2, bf16[512,256]{1,0:T(8,128)(2,1)} %k_ref.2, pred[]{:T(512)S(6)} %eq.211, pred[]{:T(512)S(6)} %eq.210, ...), kind=kLoop, calls=%fused_computation.2 | loop fusion | flops 393216 | bytes 1310723 | tf_op jit(solution)/shard_map/anchor_step1/jit(_where)/select_n | solution.py:283
  19.4 4.2 %collective-permute-start.5 = (bf16[512,256]{1,0:T(8,128)(2,1)S(1)}, bf16[512,256]{1,0:T(8,128)(2,1)S(1)}, u32[]{:S(2)}, u32[]{:S(2)}) collective-permute-start(bf16[512,256]{1,0:T(8,128)(2,1)S(1)} %select_select_fusion.2), channel_id=1, source_target_pairs={{0,64},{128,192},{4,20},{36,52},{1,65},{129,193},{5,21},{37,53},{2... | collective-permute-start | bytes 786440 | tf_op jit(solution)/shard_map/anchor_step2/ppermute | solution.py:278
  23.6 1.5 %collective-permute-start.4 = (bf16[512,256]{1,0:T(8,128)(2,1)S(1)}, bf16[512,256]{1,0:T(8,128)(2,1)S(1)}, u32[]{:S(2)}, u32[]{:S(2)}) collective-permute-start(bf16[512,256]{1,0:T(8,128)(2,1)S(1)} %select_select_fusion.2), channel_id=1, source_target_pairs={{0,32},{128,160},{4,132},{36,164},{1,33},{129,161},{5,133},{37,165... | collective-permute-start | bytes 786440 | tf_op jit(solution)/shard_map/anchor_step2/ppermute | solution.py:278
  25.1 2.5 %collective-permute-start.3 = (bf16[512,256]{1,0:T(8,128)(2,1)S(1)}, bf16[512,256]{1,0:T(8,128)(2,1)S(1)}, u32[]{:S(2)}, u32[]{:S(2)}) collective-permute-start(bf16[512,256]{1,0:T(8,128)(2,1)S(1)} %select_select_fusion.2), channel_id=1, source_target_pairs={{0,96},{128,224},{4,148},{36,180},{1,97},{129,225},{5,149},{37,181... | collective-permute-start | bytes 786440 | tf_op jit(solution)/shard_map/anchor_step2/ppermute | solution.py:278
  27.6 2.9 %all-to-all-done.q_ref = bf16[64,16,128]{2,1,0:T(8,128)(2,1)S(1)} async-done(((bf16[64,16,128]{2,1,0:T(8,128)(2,1)}), bf16[64,16,128]{2,1,0:T(8,128)(2,1)S(1)}, u32[]{:S(2)}, u32[]{:S(2)}) %all-to-all-start) | async-done | bytes 262176 | tf_op jit(solution)/shard_map/rows_out/all_to_all | solution.py:304
  30.5 2.8 %decode_part.1 = bf16[16,4,2176]{2,1,0:T(4,128)(2,1)} custom-call(s32[64]{0:T(128)S(1)} %copy-done.4, bf16[64,16,128]{2,1,0:T(8,128)(2,1)S(1)} %all-to-all-done.q_ref, bf16[512,256]{1,0:T(8,128)(2,1)S(1)} %copy-done.1, bf16[512,256]{1,0:T(8,128)(2,1)S(1)} %copy-done.2), custom_call_target="tpu_custom_call" | custom-call | flops 268435456 | bytes 1048576 | tf_op jit(solution)/shard_map/decode_part/pallas_call | solution.py:199
  33.2 4.8 %all-to-all-start.1 = ((bf16[16,4,2176]{2,1,0:T(4,128)(2,1)}), bf16[16,4,2176]{2,1,0:T(4,128)(2,1)S(1)}, u32[]{:S(2)}, u32[]{:S(2)}) async-start(bf16[16,4,2176]{2,1,0:T(4,128)(2,1)} %decode_part.1), calls=%async_computation.1 | async-start | bytes 557056 | tf_op jit(solution)/shard_map/parts_near/all_to_all | solution.py:307
  38.1 0.0 collective-permute-done.4
  38.1 0.0 collective-permute-done.3
  38.1 0.1 select_select_fusion.1
  38.2 3.3 %collective-permute-start.8 = (bf16[512,256]{1,0:T(8,128)(2,1)S(1)}, bf16[512,256]{1,0:T(8,128)(2,1)S(1)}, u32[]{:S(2)}, u32[]{:S(2)}) collective-permute-start(bf16[512,256]{1,0:T(8,128)(2,1)S(1)} %select_select_fusion.1), channel_id=1, source_target_pairs={{0,8},{32,40},{64,72},{96,104},{128,136},{160,168},{192,200},{224,... | collective-permute-start | bytes 786440 | tf_op jit(solution)/shard_map/anchor_step3/ppermute | solution.py:278
  41.5 1.3 %collective-permute-start.7 = (bf16[512,256]{1,0:T(8,128)(2,1)S(1)}, bf16[512,256]{1,0:T(8,128)(2,1)S(1)}, u32[]{:S(2)}, u32[]{:S(2)}) collective-permute-start(bf16[512,256]{1,0:T(8,128)(2,1)S(1)} %select_select_fusion.1), channel_id=1, source_target_pairs={{0,56},{32,24},{64,120},{96,88},{128,184},{160,152},{192,248},{224... | collective-permute-start | bytes 786440 | tf_op jit(solution)/shard_map/anchor_step3/ppermute | solution.py:278
  42.8 1.3 %collective-permute-start.6 = (bf16[512,256]{1,0:T(8,128)(2,1)S(1)}, bf16[512,256]{1,0:T(8,128)(2,1)S(1)}, u32[]{:S(2)}, u32[]{:S(2)}) collective-permute-start(bf16[512,256]{1,0:T(8,128)(2,1)S(1)} %select_select_fusion.1), channel_id=1, source_target_pairs={{0,16},{32,48},{64,80},{96,112},{128,144},{160,176},{192,208},{224... | collective-permute-start | bytes 786440 | tf_op jit(solution)/shard_map/anchor_step3/ppermute | solution.py:278
  44.1 1.3 %all-to-all-done.1.in_ref = bf16[16,4,2176]{2,1,0:T(4,128)(2,1)S(1)} async-done(((bf16[16,4,2176]{2,1,0:T(4,128)(2,1)}), bf16[16,4,2176]{2,1,0:T(4,128)(2,1)S(1)}, u32[]{:S(2)}, u32[]{:S(2)}) %all-to-all-start.1) | async-done | bytes 278560 | tf_op jit(solution)/shard_map/parts_near/all_to_all | solution.py:307
  45.4 1.0 %merge_parts.2 = bf16[4,4,2176]{2,1,0:T(4,128)(2,1)} custom-call(bf16[16,4,2176]{2,1,0:T(4,128)(2,1)S(1)} %all-to-all-done.1.in_ref), custom_call_target="tpu_custom_call" | custom-call | flops 1048576 | bytes 524288 | tf_op jit(solution)/shard_map/merge_parts/pallas_call | solution.py:241
  46.4 3.3 %all-to-all-start.2 = ((bf16[4,4,2176]{2,1,0:T(4,128)(2,1)}), bf16[4,4,2176]{2,1,0:T(4,128)(2,1)S(1)}, u32[]{:S(2)}, u32[]{:S(2)}) async-start(bf16[4,4,2176]{2,1,0:T(4,128)(2,1)} %merge_parts.2), calls=%async_computation.2 | async-start | bytes 139264 | tf_op jit(solution)/shard_map/parts_far/all_to_all | solution.py:311
  49.9 6.8 %all-to-all-done.2.in_ref = bf16[4,4,2176]{2,1,0:T(4,128)(2,1)S(1)} async-done(((bf16[4,4,2176]{2,1,0:T(4,128)(2,1)}), bf16[4,4,2176]{2,1,0:T(4,128)(2,1)S(1)}, u32[]{:S(2)}, u32[]{:S(2)}) %all-to-all-start.2) | async-done | bytes 69664 | tf_op jit(solution)/shard_map/parts_far/all_to_all | solution.py:311
  56.8 1.0 %merge_parts.3 = bf16[16,4,2048]{2,1,0:T(4,128)(2,1)} custom-call(bf16[4,4,2176]{2,1,0:T(4,128)(2,1)S(1)} %all-to-all-done.2.in_ref), custom_call_target="tpu_custom_call" | custom-call | flops 1048576 | bytes 524288 | tf_op jit(solution)/shard_map/merge_parts/pallas_call | solution.py:241
  57.7 5.7 %all-to-all-start.3 = ((bf16[16,4,2048]{2,1,0:T(4,128)(2,1)}), bf16[16,4,2048]{2,1,0:T(4,128)(2,1)S(1)}, u32[]{:S(2)}, u32[]{:S(2)}) async-start(bf16[16,4,2048]{2,1,0:T(4,128)(2,1)} %merge_parts.3), calls=%async_computation.3 | async-start | bytes 524288 | tf_op jit(solution)/shard_map/attn_near/all_to_all | solution.py:314
  63.4 0.0 collective-permute-done.7
  63.4 0.0 collective-permute-done.6
  63.5 0.1 select_select_fusion.one_ref
  63.5 0.2 collective-permute-start.9
  63.7 1.4 %collective-permute-done.9.two_ref = bf16[512,256]{1,0:T(8,128)(2,1)S(1)} collective-permute-done((bf16[512,256]{1,0:T(8,128)(2,1)S(1)}, bf16[512,256]{1,0:T(8,128)(2,1)S(1)}, u32[]{:S(2)}, u32[]{:S(2)}) %collective-permute-start.9) | collective-permute-done | bytes 262176 | tf_op jit(solution)/shard_map/anchor_swap/ppermute | solution.py:278
  65.2 0.7 copy-done.6
  65.9 7.6 %block_pass.2.rest_0_ = bf16[512,2048]{1,0:T(8,128)(2,1)} custom-call(s32[64]{0:T(128)} %lens.5, bf16[512,2048]{1,0:T(8,128)(2,1)} %q_ref.3, bf16[512,256]{1,0:T(8,128)(2,1)} %k_ref.2, bf16[512,256]{1,0:T(8,128)(2,1)} %v_ref.2, bf16[512,256]{1,0:T(8,128)(2,1)} %copy-done.5, bf16[512,256]{1,0:T(8,128)(2,1)} %copy-done.6), custom_call_target="tpu_custom_call" | custom-call | flops 2147483648 | bytes 4194304 | tf_op jit(solution)/shard_map/block_pass/pallas_call | solution.py:124
  73.5 0.1 reshape.7
  73.5 0.2 fusion
  73.8 2.8 %collective-permute-start.12 = (f32[64,128]{1,0:T(8,128)S(1)}, f32[64,128]{1,0:T(8,128)S(1)}, u32[]{:S(2)}, u32[]{:S(2)}) collective-permute-start(f32[64,128]{1,0:T(8,128)S(1)} %fusion), channel_id=1, source_target_pairs={{0,3},{1,2},{2,1},{3,0},{4,7},{5,6},{6,5},{7,4},{8,11},{9,10},{10,... | collective-permute-start | bytes 98312 | tf_op jit(solution)/shard_map/tp_sum/ppermute | solution.py:317
  76.6 0.3 collective-permute-start.11
  76.9 0.3 collective-permute-start.10
  77.3 7.4 %block_pass.3 = bf16[512,2048]{1,0:T(8,128)(2,1)} custom-call(s32[64]{0:T(128)} %lens.5, bf16[512,2048]{1,0:T(8,128)(2,1)} %q_ref.3, bf16[512,256]{1,0:T(8,128)(2,1)} %k_ref.2, bf16[512,256]{1,0:T(8,128)(2,1)} %v_ref.2, bf16[512,256]{1,0:T(8,128)(2,1)} %copy-done.5, bf16[512,256]{1,0:T(8,128)(2,1)} %copy-done.6, ...), custom_call_target="tpu_custom_call", output_to_operand_aliasing={{}: (6, {})} | custom-call | flops 2147483648 | bytes 4194304 | tf_op jit(solution)/shard_map/block_pass/pallas_call | solution.py:124
  84.7 0.0 collective-permute-done.12
  84.7 0.0 collective-permute-done.11
  84.7 0.0 collective-permute-done.10
  84.7 0.6 add_convert_fusion
  (12 shorter events, 0.0 us)
Async XLA Ops:
  0.6 72.9 %copy-start = (bf16[2048,128]{1,0:T(8,128)(2,1)S(1)}, bf16[2048,128]{1,0:T(8,128)(2,1)}, u32[]{:S(2)}) copy-start(bf16[2048,128]{1,0:T(8,128)(2,1)} %param.11) | copy-start | bytes 1572868
  0.6 29.8 %copy-start.2 = (bf16[512,256]{1,0:T(8,128)(2,1)S(1)}, bf16[512,256]{1,0:T(8,128)(2,1)}, u32[]{:S(2)}) copy-start(bf16[512,256]{1,0:T(8,128)(2,1)} %v_ref.2) | copy-start | bytes 786436
  0.7 29.8 %copy-start.1 = (bf16[512,256]{1,0:T(8,128)(2,1)S(1)}, bf16[512,256]{1,0:T(8,128)(2,1)}, u32[]{:S(2)}) copy-start(bf16[512,256]{1,0:T(8,128)(2,1)} %k_ref.2) | copy-start | bytes 786436
  0.7 0.8 copy-start.3
  1.4 29.0 %copy-start.4 = (s32[64]{0:T(128)S(1)}, s32[64]{0:T(128)}, u32[]{:S(2)}) copy-start(s32[64]{0:T(128)} %lens.5) | copy-start | bytes 772
  2.2 16.1 %collective-permute-start.1 = (bf16[512,256]{1,0:T(8,128)(2,1)}, bf16[512,256]{1,0:T(8,128)(2,1)S(1)}, u32[]{:S(2)}, u32[]{:S(2)}) collective-permute-start(bf16[512,256]{1,0:T(8,128)(2,1)} %v_ref.2), channel_id=1, source_target_pairs={{0,4},{1,5},{2,6},{3,7}} | collective-permute-start | bytes 786440 | tf_op jit(solution)/shard_map/anchor_step1/ppermute | solution.py:278
  3.5 14.9 %collective-permute-start = (bf16[512,256]{1,0:T(8,128)(2,1)}, bf16[512,256]{1,0:T(8,128)(2,1)S(1)}, u32[]{:S(2)}, u32[]{:S(2)}) collective-permute-start(bf16[512,256]{1,0:T(8,128)(2,1)} %v_ref.2), channel_id=1, source_target_pairs={{0,36},{1,37},{2,38},{3,39}} | collective-permute-start | bytes 786440 | tf_op jit(solution)/shard_map/anchor_step1/ppermute | solution.py:278
  4.2 14.2 %collective-permute-start.2 = (bf16[512,256]{1,0:T(8,128)(2,1)}, bf16[512,256]{1,0:T(8,128)(2,1)S(1)}, u32[]{:S(2)}, u32[]{:S(2)}) collective-permute-start(bf16[512,256]{1,0:T(8,128)(2,1)} %k_ref.2), channel_id=1, source_target_pairs={{0,128},{1,129},{2,130},{3,131}} | collective-permute-start | bytes 786440 | tf_op jit(solution)/shard_map/anchor_step1/ppermute | solution.py:278
  4.8 25.6 %all-to-all-start = ((bf16[64,16,128]{2,1,0:T(8,128)(2,1)}), bf16[64,16,128]{2,1,0:T(8,128)(2,1)S(1)}, u32[]{:S(2)}, u32[]{:S(2)}) async-start(bf16[64,16,128]{2,1,0:T(8,128)(2,1)} %spread_rows.1), calls=%async_computation | async-start | bytes 524288 | tf_op jit(solution)/shard_map/rows_out/all_to_all | solution.py:304
  19.4 18.7 %collective-permute-start.5 = (bf16[512,256]{1,0:T(8,128)(2,1)S(1)}, bf16[512,256]{1,0:T(8,128)(2,1)S(1)}, u32[]{:S(2)}, u32[]{:S(2)}) collective-permute-start(bf16[512,256]{1,0:T(8,128)(2,1)S(1)} %select_select_fusion.2), channel_id=1, source_target_pairs={{0,64},{128,192},{4,20},{36,52},{1,65},{129,193},{5,21},{37,53},{2... | collective-permute-start | bytes 786440 | tf_op jit(solution)/shard_map/anchor_step2/ppermute | solution.py:278
  23.6 14.5 %collective-permute-start.4 = (bf16[512,256]{1,0:T(8,128)(2,1)S(1)}, bf16[512,256]{1,0:T(8,128)(2,1)S(1)}, u32[]{:S(2)}, u32[]{:S(2)}) collective-permute-start(bf16[512,256]{1,0:T(8,128)(2,1)S(1)} %select_select_fusion.2), channel_id=1, source_target_pairs={{0,32},{128,160},{4,132},{36,164},{1,33},{129,161},{5,133},{37,165... | collective-permute-start | bytes 786440 | tf_op jit(solution)/shard_map/anchor_step2/ppermute | solution.py:278
  25.1 13.0 %collective-permute-start.3 = (bf16[512,256]{1,0:T(8,128)(2,1)S(1)}, bf16[512,256]{1,0:T(8,128)(2,1)S(1)}, u32[]{:S(2)}, u32[]{:S(2)}) collective-permute-start(bf16[512,256]{1,0:T(8,128)(2,1)S(1)} %select_select_fusion.2), channel_id=1, source_target_pairs={{0,96},{128,224},{4,148},{36,180},{1,97},{129,225},{5,149},{37,181... | collective-permute-start | bytes 786440 | tf_op jit(solution)/shard_map/anchor_step2/ppermute | solution.py:278
  33.2 12.1 %all-to-all-start.1 = ((bf16[16,4,2176]{2,1,0:T(4,128)(2,1)}), bf16[16,4,2176]{2,1,0:T(4,128)(2,1)S(1)}, u32[]{:S(2)}, u32[]{:S(2)}) async-start(bf16[16,4,2176]{2,1,0:T(4,128)(2,1)} %decode_part.1), calls=%async_computation.1 | async-start | bytes 557056 | tf_op jit(solution)/shard_map/parts_near/all_to_all | solution.py:307
  38.2 25.3 %collective-permute-start.8 = (bf16[512,256]{1,0:T(8,128)(2,1)S(1)}, bf16[512,256]{1,0:T(8,128)(2,1)S(1)}, u32[]{:S(2)}, u32[]{:S(2)}) collective-permute-start(bf16[512,256]{1,0:T(8,128)(2,1)S(1)} %select_select_fusion.1), channel_id=1, source_target_pairs={{0,8},{32,40},{64,72},{96,104},{128,136},{160,168},{192,200},{224,... | collective-permute-start | bytes 786440 | tf_op jit(solution)/shard_map/anchor_step3/ppermute | solution.py:278
  41.5 22.0 %collective-permute-start.7 = (bf16[512,256]{1,0:T(8,128)(2,1)S(1)}, bf16[512,256]{1,0:T(8,128)(2,1)S(1)}, u32[]{:S(2)}, u32[]{:S(2)}) collective-permute-start(bf16[512,256]{1,0:T(8,128)(2,1)S(1)} %select_select_fusion.1), channel_id=1, source_target_pairs={{0,56},{32,24},{64,120},{96,88},{128,184},{160,152},{192,248},{224... | collective-permute-start | bytes 786440 | tf_op jit(solution)/shard_map/anchor_step3/ppermute | solution.py:278
  42.8 20.7 %collective-permute-start.6 = (bf16[512,256]{1,0:T(8,128)(2,1)S(1)}, bf16[512,256]{1,0:T(8,128)(2,1)S(1)}, u32[]{:S(2)}, u32[]{:S(2)}) collective-permute-start(bf16[512,256]{1,0:T(8,128)(2,1)S(1)} %select_select_fusion.1), channel_id=1, source_target_pairs={{0,16},{32,48},{64,80},{96,112},{128,144},{160,176},{192,208},{224... | collective-permute-start | bytes 786440 | tf_op jit(solution)/shard_map/anchor_step3/ppermute | solution.py:278
  46.4 10.4 %all-to-all-start.2 = ((bf16[4,4,2176]{2,1,0:T(4,128)(2,1)}), bf16[4,4,2176]{2,1,0:T(4,128)(2,1)S(1)}, u32[]{:S(2)}, u32[]{:S(2)}) async-start(bf16[4,4,2176]{2,1,0:T(4,128)(2,1)} %merge_parts.2), calls=%async_computation.2 | async-start | bytes 139264 | tf_op jit(solution)/shard_map/parts_far/all_to_all | solution.py:311
  57.7 15.7 %all-to-all-start.3 = ((bf16[16,4,2048]{2,1,0:T(4,128)(2,1)}), bf16[16,4,2048]{2,1,0:T(4,128)(2,1)S(1)}, u32[]{:S(2)}, u32[]{:S(2)}) async-start(bf16[16,4,2048]{2,1,0:T(4,128)(2,1)} %merge_parts.3), calls=%async_computation.3 | async-start | bytes 524288 | tf_op jit(solution)/shard_map/attn_near/all_to_all | solution.py:314
  63.5 1.6 %copy-start.5 = (bf16[512,256]{1,0:T(8,128)(2,1)}, bf16[512,256]{1,0:T(8,128)(2,1)S(1)}, u32[]{:S(2)}) copy-start(bf16[512,256]{1,0:T(8,128)(2,1)S(1)} %select_select_fusion.one_ref) | copy-start | bytes 786436
  63.5 1.6 %collective-permute-start.9 = (bf16[512,256]{1,0:T(8,128)(2,1)S(1)}, bf16[512,256]{1,0:T(8,128)(2,1)S(1)}, u32[]{:S(2)}, u32[]{:S(2)}) collective-permute-start(bf16[512,256]{1,0:T(8,128)(2,1)S(1)} %select_select_fusion.one_ref), channel_id=1, source_target_pairs={{0,4},{4,0},{8,12},{12,8},{16,20},{20,16},{24,28},{28,24},{32,36},... | collective-permute-start | bytes 786440 | tf_op jit(solution)/shard_map/anchor_swap/ppermute | solution.py:278
  65.1 0.7 copy-start.6
  73.8 10.9 %collective-permute-start.12 = (f32[64,128]{1,0:T(8,128)S(1)}, f32[64,128]{1,0:T(8,128)S(1)}, u32[]{:S(2)}, u32[]{:S(2)}) collective-permute-start(f32[64,128]{1,0:T(8,128)S(1)} %fusion), channel_id=1, source_target_pairs={{0,3},{1,2},{2,1},{3,0},{4,7},{5,6},{6,5},{7,4},{8,11},{9,10},{10,... | collective-permute-start | bytes 98312 | tf_op jit(solution)/shard_map/tp_sum/ppermute | solution.py:317
  76.6 8.1 %collective-permute-start.11 = (f32[64,128]{1,0:T(8,128)S(1)}, f32[64,128]{1,0:T(8,128)S(1)}, u32[]{:S(2)}, u32[]{:S(2)}) collective-permute-start(f32[64,128]{1,0:T(8,128)S(1)} %fusion), channel_id=1, source_target_pairs={{0,2},{1,3},{2,0},{3,1},{4,6},{5,7},{6,4},{7,5},{8,10},{9,11},{10,... | collective-permute-start | bytes 98312 | tf_op jit(solution)/shard_map/tp_sum/ppermute | solution.py:317
  76.9 7.8 %collective-permute-start.10 = (f32[64,128]{1,0:T(8,128)S(1)}, f32[64,128]{1,0:T(8,128)S(1)}, u32[]{:S(2)}, u32[]{:S(2)}) collective-permute-start(f32[64,128]{1,0:T(8,128)S(1)} %fusion), channel_id=1, source_target_pairs={{0,1},{1,0},{2,3},{3,2},{4,5},{5,4},{6,7},{7,6},{8,9},{9,8},{10,11... | collective-permute-start | bytes 98312 | tf_op jit(solution)/shard_map/tp_sum/ppermute | solution.py:317

commit v3 on v2

--- a/solution.py
+++ b/solution.py
@@ -250,15 +250,13 @@
 
 
 def anchor_moves():
-    near = [(0, 0), (1, 0), (0, 4), (1, 4)]
-    keys_2 = [
-        [((x, 0), (x + dx, dz)) for x in (0, 2)] for dx, dz in near[1:]
-    ]
+    keys_2 = [[((x, 0), (x + dx, dz)) for x in (0, 2)] for dx, dz in ((1, 0), (0, 3), (1, 3))]
     values_2 = [
-        [((0, z), (dx, z + dz)) for z in (0, 4)] for dx, dz in ((0, 2), (2, 0), (2, 2))
+        [((0, 0), (dx, -dz % NZ)), ((0, 2), (dx, 2 + dz))] for dx, dz in ((0, 2), (2, 0), (2, 2))
     ]
     keys_3 = [
-        [((x, z), (x, (z + dz) % NZ)) for x in range(NX) for z in (0, 4)] for dz in (1, -1, 2)
+        [((x, 0), (x, near)) for x in range(NX)] + [((x, 3), (x, far)) for x in range(NX)]
+        for near, far in ((1, 2), (7, 4), (6, 5))
     ]
     values_3 = [
         [((x, z), (x + dx, z + dz)) for x in (0, 2) for z in (0, 2, 4, 6)] for dx, dz in ((1, 0), (0, 1), (1, 1))
@@ -285,7 +283,7 @@
 
     with jax.named_scope("anchor_step1"):
         root = ctx_at(0, 0, 0)
-        moves = [[(root, ctx_at(2, 0, 0))], [(root, ctx_at(0, 0, 1))], [(root, ctx_at(0, 4, 1))]]
+        moves = [[(root, ctx_at(2, 0, 0))], [(root, ctx_at(0, 0, 1))], [(root, ctx_at(0, 2, 1))]]
         held = place(keys, [perm(block, pairs) for block, pairs in zip((keys, values, values), moves)], moves)
     for number, moves in enumerate(anchor_moves()):
         with jax.named_scope(f"anchor_step{number + 2}"):

time: 86 us -> 84.6 us (0.984)
  waiting for transfers between devices: 12.5 us -> 11 us
    all_to_all x1, waiting for transfers between devices: 2.86 us -> 1.55 us  [body(): rows = lax.all_to_all(copies, 'ctx', 0, 0, tiled=True)]
    ppermute x10, starting transfers between devices: 16.9 us -> 18.2 us  [fetch_anchor(): perm = lambda block, pairs: lax.ppermute(block, 'ctx', pairs)]
    all_to_all x1, starting transfers between devices: 13.5 us -> 12.4 us  [body(): rows = lax.all_to_all(copies, 'ctx', 0, 0, tiled=True)]
  transfers between devices with their start and end apart: 17 -> 17, of which waited for: 4 -> 4; matrix products, arithmetic and copies ran while one was open for 1% -> 1% of each run, Pallas kernels for 23% -> 24%
where the time goes in v3:
time: 84.6 us; the launch traced here: 83.9 us
  starting transfers between devices  47.7 us (56%)
  Pallas kernels  20.5 us (24%)
  waiting for transfers between devices  11 us (13%)
  other arithmetic  1.76 us (2%)
  local copies, waits for them, and re-layouts  1.57 us (2%)
  between operations  1.14 us (1%)
    ppermute x10, starting transfers between devices, fetch_anchor(): perm = lambda block, pairs: lax.ppermute(block, 'ctx', pairs)  18.2 us
    pallas_call x2, Pallas kernels, block_pass(): pl.pallas_call(functools.partial(block_kernel, step), grid_spec=pltpu.Pre...  15 us
    all_to_all x1, starting transfers between devices, body(): rows = lax.all_to_all(copies, 'ctx', 0, 0, tiled=True)  12.4 us
    all_to_all x1, waiting for transfers between devices, body(): lax.all_to_all(merged, 'ctx', 0, 0, axis_index_groups=FAR_GROUPS, tiled=T...  6.83 us
    all_to_all x1, starting transfers between devices, body(): lax.all_to_all(attn, 'ctx', 0, 0, axis_index_groups=NEAR_GROUPS, tiled=True)  5.45 us
    all_to_all x1, starting transfers between devices, body(): lax.all_to_all(message, 'ctx', 0, 0, axis_index_groups=NEAR_GROUPS, tiled...  4.88 us
    ppermute x3, starting transfers between devices, body(): lax.ppermute(projected, 'tp', [(i, i ^ k) for i in range(NTP)])  3.5 us
    all_to_all x1, starting transfers between devices, body(): lax.all_to_all(merged, 'ctx', 0, 0, axis_index_groups=FAR_GROUPS, tiled=T...  3.29 us
  transfers between devices with their start and end apart: 17, of which 4 were waited for; matrix products, arithmetic and copies ran while one was open for 1% of the time, Pallas kernels for 24%

profile of v3, /device:TPU:1, one launch (start us, length us, event | category | flops | bytes accessed | tf_op | source)
XLA Modules:
  0.0 83.9 jit_solution(12196782636293867428)
XLA Ops:
  0.6 0.0 copy-start
  0.6 0.0 copy-start.2
  0.7 0.0 copy-start.1
  0.7 0.8 copy-done.3
  1.5 0.7 spread_rows.1
  2.2 1.3 %collective-permute-start.1 = (bf16[512,256]{1,0:T(8,128)(2,1)}, bf16[512,256]{1,0:T(8,128)(2,1)S(1)}, u32[]{:S(2)}, u32[]{:S(2)}) collective-permute-start(bf16[512,256]{1,0:T(8,128)(2,1)} %v_ref.2), channel_id=1, source_target_pairs={{0,4},{1,5},{2,6},{3,7}} | collective-permute-start | bytes 786440 | tf_op jit(solution)/shard_map/anchor_step1/ppermute | solution.py:276
  3.5 0.7 collective-permute-start
  4.2 0.7 collective-permute-start.2
  4.8 12.4 %all-to-all-start = ((bf16[64,16,128]{2,1,0:T(8,128)(2,1)}), bf16[64,16,128]{2,1,0:T(8,128)(2,1)S(1)}, u32[]{:S(2)}, u32[]{:S(2)}) async-start(bf16[64,16,128]{2,1,0:T(8,128)(2,1)} %spread_rows.1), calls=%async_computation | async-start | bytes 524288 | tf_op jit(solution)/shard_map/rows_out/all_to_all | solution.py:302
  17.2 0.0 collective-permute-done.1
  17.2 0.0 collective-permute-done
  17.3 0.0 collective-permute-done.2
  17.3 1.0 %select_select_fusion.2 = bf16[512,256]{1,0:T(8,128)(2,1)S(1)} fusion(bf16[512,256]{1,0:T(8,128)(2,1)S(1)} %collective-permute-done, bf16[512,256]{1,0:T(8,128)(2,1)S(1)} %collective-permute-done.1, bf16[512,256]{1,0:T(8,128)(2,1)S(1)} %collective-permute-done.2, bf16[512,256]{1,0:T(8,128)(2,1)} %k_ref.2, pred[]{:T(512)S(6)} %eq.211, pred[]{:T(512)S(6)} %eq.210, ...), kind=kLoop, calls=%fused_computation.2 | loop fusion | flops 393216 | bytes 1310723 | tf_op jit(solution)/shard_map/anchor_step1/jit(_where)/select_n | solution.py:281
  18.3 5.4 %collective-permute-start.5 = (bf16[512,256]{1,0:T(8,128)(2,1)S(1)}, bf16[512,256]{1,0:T(8,128)(2,1)S(1)}, u32[]{:S(2)}, u32[]{:S(2)}) collective-permute-start(bf16[512,256]{1,0:T(8,128)(2,1)S(1)} %select_select_fusion.2), channel_id=1, source_target_pairs={{0,64},{128,192},{4,52},{20,36},{1,65},{129,193},{5,53},{21,37},{2... | collective-permute-start | bytes 786440 | tf_op jit(solution)/shard_map/anchor_step2/ppermute | solution.py:276
  23.7 1.3 %collective-permute-start.4 = (bf16[512,256]{1,0:T(8,128)(2,1)S(1)}, bf16[512,256]{1,0:T(8,128)(2,1)S(1)}, u32[]{:S(2)}, u32[]{:S(2)}) collective-permute-start(bf16[512,256]{1,0:T(8,128)(2,1)S(1)} %select_select_fusion.2), channel_id=1, source_target_pairs={{0,24},{128,152},{4,132},{20,148},{1,25},{129,153},{5,133},{21,149... | collective-permute-start | bytes 786440 | tf_op jit(solution)/shard_map/anchor_step2/ppermute | solution.py:276
  25.0 2.6 %collective-permute-start.3 = (bf16[512,256]{1,0:T(8,128)(2,1)S(1)}, bf16[512,256]{1,0:T(8,128)(2,1)S(1)}, u32[]{:S(2)}, u32[]{:S(2)}) collective-permute-start(bf16[512,256]{1,0:T(8,128)(2,1)S(1)} %select_select_fusion.2), channel_id=1, source_target_pairs={{0,88},{128,216},{4,180},{20,164},{1,89},{129,217},{5,181},{21,165... | collective-permute-start | bytes 786440 | tf_op jit(solution)/shard_map/anchor_step2/ppermute | solution.py:276
  27.7 1.5 %all-to-all-done.q_ref = bf16[64,16,128]{2,1,0:T(8,128)(2,1)S(1)} async-done(((bf16[64,16,128]{2,1,0:T(8,128)(2,1)}), bf16[64,16,128]{2,1,0:T(8,128)(2,1)S(1)}, u32[]{:S(2)}, u32[]{:S(2)}) %all-to-all-start) | async-done | bytes 262176 | tf_op jit(solution)/shard_map/rows_out/all_to_all | solution.py:302
  29.2 2.8 %decode_part.1 = bf16[16,4,2176]{2,1,0:T(4,128)(2,1)} custom-call(s32[64]{0:T(128)S(1)} %copy-done.4, bf16[64,16,128]{2,1,0:T(8,128)(2,1)S(1)} %all-to-all-done.q_ref, bf16[512,256]{1,0:T(8,128)(2,1)S(1)} %copy-done.1, bf16[512,256]{1,0:T(8,128)(2,1)S(1)} %copy-done.2), custom_call_target="tpu_custom_call" | custom-call | flops 268435456 | bytes 1048576 | tf_op jit(solution)/shard_map/decode_part/pallas_call | solution.py:199
  32.0 4.9 %all-to-all-start.1 = ((bf16[16,4,2176]{2,1,0:T(4,128)(2,1)}), bf16[16,4,2176]{2,1,0:T(4,128)(2,1)S(1)}, u32[]{:S(2)}, u32[]{:S(2)}) async-start(bf16[16,4,2176]{2,1,0:T(4,128)(2,1)} %decode_part.1), calls=%async_computation.1 | async-start | bytes 557056 | tf_op jit(solution)/shard_map/parts_near/all_to_all | solution.py:305
  36.9 0.0 collective-permute-done.5
  36.9 0.0 collective-permute-done.4
  36.9 0.0 collective-permute-done.3
  36.9 0.1 select_select_fusion.1
  37.0 3.3 %collective-permute-start.8 = (bf16[512,256]{1,0:T(8,128)(2,1)S(1)}, bf16[512,256]{1,0:T(8,128)(2,1)S(1)}, u32[]{:S(2)}, u32[]{:S(2)}) collective-permute-start(bf16[512,256]{1,0:T(8,128)(2,1)S(1)} %select_select_fusion.1), channel_id=1, source_target_pairs={{0,8},{64,72},{128,136},{192,200},{24,16},{88,80},{152,144},{216,2... | collective-permute-start | bytes 786440 | tf_op jit(solution)/shard_map/anchor_step3/ppermute | solution.py:276
  40.3 1.3 %collective-permute-start.7 = (bf16[512,256]{1,0:T(8,128)(2,1)S(1)}, bf16[512,256]{1,0:T(8,128)(2,1)S(1)}, u32[]{:S(2)}, u32[]{:S(2)}) collective-permute-start(bf16[512,256]{1,0:T(8,128)(2,1)S(1)} %select_select_fusion.1), channel_id=1, source_target_pairs={{0,56},{64,120},{128,184},{192,248},{24,32},{88,96},{152,160},{216... | collective-permute-start | bytes 786440 | tf_op jit(solution)/shard_map/anchor_step3/ppermute | solution.py:276
  41.6 1.3 %collective-permute-start.6 = (bf16[512,256]{1,0:T(8,128)(2,1)S(1)}, bf16[512,256]{1,0:T(8,128)(2,1)S(1)}, u32[]{:S(2)}, u32[]{:S(2)}) collective-permute-start(bf16[512,256]{1,0:T(8,128)(2,1)S(1)} %select_select_fusion.1), channel_id=1, source_target_pairs={{0,48},{64,112},{128,176},{192,240},{24,40},{88,104},{152,168},{21... | collective-permute-start | bytes 786440 | tf_op jit(solution)/shard_map/anchor_step3/ppermute | solution.py:276
  42.9 1.3 %all-to-all-done.1.in_ref = bf16[16,4,2176]{2,1,0:T(4,128)(2,1)S(1)} async-done(((bf16[16,4,2176]{2,1,0:T(4,128)(2,1)}), bf16[16,4,2176]{2,1,0:T(4,128)(2,1)S(1)}, u32[]{:S(2)}, u32[]{:S(2)}) %all-to-all-start.1) | async-done | bytes 278560 | tf_op jit(solution)/shard_map/parts_near/all_to_all | solution.py:305
  44.2 1.0 %merge_parts.2 = bf16[4,4,2176]{2,1,0:T(4,128)(2,1)} custom-call(bf16[16,4,2176]{2,1,0:T(4,128)(2,1)S(1)} %all-to-all-done.1.in_ref), custom_call_target="tpu_custom_call" | custom-call | flops 1048576 | bytes 524288 | tf_op jit(solution)/shard_map/merge_parts/pallas_call | solution.py:241
  45.2 3.3 %all-to-all-start.2 = ((bf16[4,4,2176]{2,1,0:T(4,128)(2,1)}), bf16[4,4,2176]{2,1,0:T(4,128)(2,1)S(1)}, u32[]{:S(2)}, u32[]{:S(2)}) async-start(bf16[4,4,2176]{2,1,0:T(4,128)(2,1)} %merge_parts.2), calls=%async_computation.2 | async-start | bytes 139264 | tf_op jit(solution)/shard_map/parts_far/all_to_all | solution.py:309
  48.7 6.8 %all-to-all-done.2.in_ref = bf16[4,4,2176]{2,1,0:T(4,128)(2,1)S(1)} async-done(((bf16[4,4,2176]{2,1,0:T(4,128)(2,1)}), bf16[4,4,2176]{2,1,0:T(4,128)(2,1)S(1)}, u32[]{:S(2)}, u32[]{:S(2)}) %all-to-all-start.2) | async-done | bytes 69664 | tf_op jit(solution)/shard_map/parts_far/all_to_all | solution.py:309
  55.5 1.0 %merge_parts.3 = bf16[16,4,2048]{2,1,0:T(4,128)(2,1)} custom-call(bf16[4,4,2176]{2,1,0:T(4,128)(2,1)S(1)} %all-to-all-done.2.in_ref), custom_call_target="tpu_custom_call" | custom-call | flops 1048576 | bytes 524288 | tf_op jit(solution)/shard_map/merge_parts/pallas_call | solution.py:241
  56.5 5.5 %all-to-all-start.3 = ((bf16[16,4,2048]{2,1,0:T(4,128)(2,1)}), bf16[16,4,2048]{2,1,0:T(4,128)(2,1)S(1)}, u32[]{:S(2)}, u32[]{:S(2)}) async-start(bf16[16,4,2048]{2,1,0:T(4,128)(2,1)} %merge_parts.3), calls=%async_computation.3 | async-start | bytes 524288 | tf_op jit(solution)/shard_map/attn_near/all_to_all | solution.py:312
  62.0 0.0 collective-permute-done.8
  62.0 0.0 collective-permute-done.7
  62.0 0.0 collective-permute-done.6
  62.0 0.1 select_select_fusion.one_ref
  62.1 0.3 collective-permute-start.9
  62.4 1.3 %collective-permute-done.9.two_ref = bf16[512,256]{1,0:T(8,128)(2,1)S(1)} collective-permute-done((bf16[512,256]{1,0:T(8,128)(2,1)S(1)}, bf16[512,256]{1,0:T(8,128)(2,1)S(1)}, u32[]{:S(2)}, u32[]{:S(2)}) %collective-permute-start.9) | collective-permute-done | bytes 262176 | tf_op jit(solution)/shard_map/anchor_swap/ppermute | solution.py:276
  63.7 0.7 copy-done.6
  64.4 7.6 %block_pass.2.rest_0_ = bf16[512,2048]{1,0:T(8,128)(2,1)} custom-call(s32[64]{0:T(128)} %lens.5, bf16[512,2048]{1,0:T(8,128)(2,1)} %q_ref.3, bf16[512,256]{1,0:T(8,128)(2,1)} %k_ref.2, bf16[512,256]{1,0:T(8,128)(2,1)} %v_ref.2, bf16[512,256]{1,0:T(8,128)(2,1)} %copy-done.5, bf16[512,256]{1,0:T(8,128)(2,1)} %copy-done.6), custom_call_target="tpu_custom_call" | custom-call | flops 2147483648 | bytes 4194304 | tf_op jit(solution)/shard_map/block_pass/pallas_call | solution.py:124
  72.0 0.0 all-to-all-done.3
  72.0 0.1 reshape.7
  72.1 0.2 fusion
  72.3 2.8 %collective-permute-start.12 = (f32[64,128]{1,0:T(8,128)S(1)}, f32[64,128]{1,0:T(8,128)S(1)}, u32[]{:S(2)}, u32[]{:S(2)}) collective-permute-start(f32[64,128]{1,0:T(8,128)S(1)} %fusion), channel_id=1, source_target_pairs={{0,3},{1,2},{2,1},{3,0},{4,7},{5,6},{6,5},{7,4},{8,11},{9,10},{10,... | collective-permute-start | bytes 98312 | tf_op jit(solution)/shard_map/tp_sum/ppermute | solution.py:315
  75.1 0.3 collective-permute-start.11
  75.5 0.3 collective-permute-start.10
  75.8 7.4 %block_pass.3 = bf16[512,2048]{1,0:T(8,128)(2,1)} custom-call(s32[64]{0:T(128)} %lens.5, bf16[512,2048]{1,0:T(8,128)(2,1)} %q_ref.3, bf16[512,256]{1,0:T(8,128)(2,1)} %k_ref.2, bf16[512,256]{1,0:T(8,128)(2,1)} %v_ref.2, bf16[512,256]{1,0:T(8,128)(2,1)} %copy-done.5, bf16[512,256]{1,0:T(8,128)(2,1)} %copy-done.6, ...), custom_call_target="tpu_custom_call", output_to_operand_aliasing={{}: (6, {})} | custom-call | flops 2147483648 | bytes 4194304 | tf_op jit(solution)/shard_map/block_pass/pallas_call | solution.py:124
  83.3 0.6 add_convert_fusion
  (12 shorter events, 0.0 us)
Async XLA Ops:
  0.6 71.4 %copy-start = (bf16[2048,128]{1,0:T(8,128)(2,1)S(1)}, bf16[2048,128]{1,0:T(8,128)(2,1)}, u32[]{:S(2)}) copy-start(bf16[2048,128]{1,0:T(8,128)(2,1)} %param.11) | copy-start | bytes 1572868
  0.6 28.6 %copy-start.2 = (bf16[512,256]{1,0:T(8,128)(2,1)S(1)}, bf16[512,256]{1,0:T(8,128)(2,1)}, u32[]{:S(2)}) copy-start(bf16[512,256]{1,0:T(8,128)(2,1)} %v_ref.2) | copy-start | bytes 786436
  0.7 28.6 %copy-start.1 = (bf16[512,256]{1,0:T(8,128)(2,1)S(1)}, bf16[512,256]{1,0:T(8,128)(2,1)}, u32[]{:S(2)}) copy-start(bf16[512,256]{1,0:T(8,128)(2,1)} %k_ref.2) | copy-start | bytes 786436
  0.7 0.8 copy-start.3
  1.4 27.8 %copy-start.4 = (s32[64]{0:T(128)S(1)}, s32[64]{0:T(128)}, u32[]{:S(2)}) copy-start(s32[64]{0:T(128)} %lens.5) | copy-start | bytes 772
  2.2 15.1 %collective-permute-start.1 = (bf16[512,256]{1,0:T(8,128)(2,1)}, bf16[512,256]{1,0:T(8,128)(2,1)S(1)}, u32[]{:S(2)}, u32[]{:S(2)}) collective-permute-start(bf16[512,256]{1,0:T(8,128)(2,1)} %v_ref.2), channel_id=1, source_target_pairs={{0,4},{1,5},{2,6},{3,7}} | collective-permute-start | bytes 786440 | tf_op jit(solution)/shard_map/anchor_step1/ppermute | solution.py:276
  3.5 13.8 %collective-permute-start = (bf16[512,256]{1,0:T(8,128)(2,1)}, bf16[512,256]{1,0:T(8,128)(2,1)S(1)}, u32[]{:S(2)}, u32[]{:S(2)}) collective-permute-start(bf16[512,256]{1,0:T(8,128)(2,1)} %v_ref.2), channel_id=1, source_target_pairs={{0,20},{1,21},{2,22},{3,23}} | collective-permute-start | bytes 786440 | tf_op jit(solution)/shard_map/anchor_step1/ppermute | solution.py:276
  4.2 13.1 %collective-permute-start.2 = (bf16[512,256]{1,0:T(8,128)(2,1)}, bf16[512,256]{1,0:T(8,128)(2,1)S(1)}, u32[]{:S(2)}, u32[]{:S(2)}) collective-permute-start(bf16[512,256]{1,0:T(8,128)(2,1)} %k_ref.2), channel_id=1, source_target_pairs={{0,128},{1,129},{2,130},{3,131}} | collective-permute-start | bytes 786440 | tf_op jit(solution)/shard_map/anchor_step1/ppermute | solution.py:276
  4.8 24.4 %all-to-all-start = ((bf16[64,16,128]{2,1,0:T(8,128)(2,1)}), bf16[64,16,128]{2,1,0:T(8,128)(2,1)S(1)}, u32[]{:S(2)}, u32[]{:S(2)}) async-start(bf16[64,16,128]{2,1,0:T(8,128)(2,1)} %spread_rows.1), calls=%async_computation | async-start | bytes 524288 | tf_op jit(solution)/shard_map/rows_out/all_to_all | solution.py:302
  18.3 18.6 %collective-permute-start.5 = (bf16[512,256]{1,0:T(8,128)(2,1)S(1)}, bf16[512,256]{1,0:T(8,128)(2,1)S(1)}, u32[]{:S(2)}, u32[]{:S(2)}) collective-permute-start(bf16[512,256]{1,0:T(8,128)(2,1)S(1)} %select_select_fusion.2), channel_id=1, source_target_pairs={{0,64},{128,192},{4,52},{20,36},{1,65},{129,193},{5,53},{21,37},{2... | collective-permute-start | bytes 786440 | tf_op jit(solution)/shard_map/anchor_step2/ppermute | solution.py:276
  23.7 13.2 %collective-permute-start.4 = (bf16[512,256]{1,0:T(8,128)(2,1)S(1)}, bf16[512,256]{1,0:T(8,128)(2,1)S(1)}, u32[]{:S(2)}, u32[]{:S(2)}) collective-permute-start(bf16[512,256]{1,0:T(8,128)(2,1)S(1)} %select_select_fusion.2), channel_id=1, source_target_pairs={{0,24},{128,152},{4,132},{20,148},{1,25},{129,153},{5,133},{21,149... | collective-permute-start | bytes 786440 | tf_op jit(solution)/shard_map/anchor_step2/ppermute | solution.py:276
  25.0 11.8 %collective-permute-start.3 = (bf16[512,256]{1,0:T(8,128)(2,1)S(1)}, bf16[512,256]{1,0:T(8,128)(2,1)S(1)}, u32[]{:S(2)}, u32[]{:S(2)}) collective-permute-start(bf16[512,256]{1,0:T(8,128)(2,1)S(1)} %select_select_fusion.2), channel_id=1, source_target_pairs={{0,88},{128,216},{4,180},{20,164},{1,89},{129,217},{5,181},{21,165... | collective-permute-start | bytes 786440 | tf_op jit(solution)/shard_map/anchor_step2/ppermute | solution.py:276
  32.0 12.2 %all-to-all-start.1 = ((bf16[16,4,2176]{2,1,0:T(4,128)(2,1)}), bf16[16,4,2176]{2,1,0:T(4,128)(2,1)S(1)}, u32[]{:S(2)}, u32[]{:S(2)}) async-start(bf16[16,4,2176]{2,1,0:T(4,128)(2,1)} %decode_part.1), calls=%async_computation.1 | async-start | bytes 557056 | tf_op jit(solution)/shard_map/parts_near/all_to_all | solution.py:305
  37.0 25.0 %collective-permute-start.8 = (bf16[512,256]{1,0:T(8,128)(2,1)S(1)}, bf16[512,256]{1,0:T(8,128)(2,1)S(1)}, u32[]{:S(2)}, u32[]{:S(2)}) collective-permute-start(bf16[512,256]{1,0:T(8,128)(2,1)S(1)} %select_select_fusion.1), channel_id=1, source_target_pairs={{0,8},{64,72},{128,136},{192,200},{24,16},{88,80},{152,144},{216,2... | collective-permute-start | bytes 786440 | tf_op jit(solution)/shard_map/anchor_step3/ppermute | solution.py:276
  40.3 21.7 %collective-permute-start.7 = (bf16[512,256]{1,0:T(8,128)(2,1)S(1)}, bf16[512,256]{1,0:T(8,128)(2,1)S(1)}, u32[]{:S(2)}, u32[]{:S(2)}) collective-permute-start(bf16[512,256]{1,0:T(8,128)(2,1)S(1)} %select_select_fusion.1), channel_id=1, source_target_pairs={{0,56},{64,120},{128,184},{192,248},{24,32},{88,96},{152,160},{216... | collective-permute-start | bytes 786440 | tf_op jit(solution)/shard_map/anchor_step3/ppermute | solution.py:276
  41.6 20.4 %collective-permute-start.6 = (bf16[512,256]{1,0:T(8,128)(2,1)S(1)}, bf16[512,256]{1,0:T(8,128)(2,1)S(1)}, u32[]{:S(2)}, u32[]{:S(2)}) collective-permute-start(bf16[512,256]{1,0:T(8,128)(2,1)S(1)} %select_select_fusion.1), channel_id=1, source_target_pairs={{0,48},{64,112},{128,176},{192,240},{24,40},{88,104},{152,168},{21... | collective-permute-start | bytes 786440 | tf_op jit(solution)/shard_map/anchor_step3/ppermute | solution.py:276
  45.2 10.4 %all-to-all-start.2 = ((bf16[4,4,2176]{2,1,0:T(4,128)(2,1)}), bf16[4,4,2176]{2,1,0:T(4,128)(2,1)S(1)}, u32[]{:S(2)}, u32[]{:S(2)}) async-start(bf16[4,4,2176]{2,1,0:T(4,128)(2,1)} %merge_parts.2), calls=%async_computation.2 | async-start | bytes 139264 | tf_op jit(solution)/shard_map/parts_far/all_to_all | solution.py:309
  56.5 15.5 %all-to-all-start.3 = ((bf16[16,4,2048]{2,1,0:T(4,128)(2,1)}), bf16[16,4,2048]{2,1,0:T(4,128)(2,1)S(1)}, u32[]{:S(2)}, u32[]{:S(2)}) async-start(bf16[16,4,2048]{2,1,0:T(4,128)(2,1)} %merge_parts.3), calls=%async_computation.3 | async-start | bytes 524288 | tf_op jit(solution)/shard_map/attn_near/all_to_all | solution.py:312
  62.1 1.6 %copy-start.5 = (bf16[512,256]{1,0:T(8,128)(2,1)}, bf16[512,256]{1,0:T(8,128)(2,1)S(1)}, u32[]{:S(2)}) copy-start(bf16[512,256]{1,0:T(8,128)(2,1)S(1)} %select_select_fusion.one_ref) | copy-start | bytes 786436
  62.1 1.6 %collective-permute-start.9 = (bf16[512,256]{1,0:T(8,128)(2,1)S(1)}, bf16[512,256]{1,0:T(8,128)(2,1)S(1)}, u32[]{:S(2)}, u32[]{:S(2)}) collective-permute-start(bf16[512,256]{1,0:T(8,128)(2,1)S(1)} %select_select_fusion.one_ref), channel_id=1, source_target_pairs={{0,4},{4,0},{8,12},{12,8},{16,20},{20,16},{24,28},{28,24},{32,36},... | collective-permute-start | bytes 786440 | tf_op jit(solution)/shard_map/anchor_swap/ppermute | solution.py:276
  63.7 0.7 copy-start.6
  72.3 10.9 %collective-permute-start.12 = (f32[64,128]{1,0:T(8,128)S(1)}, f32[64,128]{1,0:T(8,128)S(1)}, u32[]{:S(2)}, u32[]{:S(2)}) collective-permute-start(f32[64,128]{1,0:T(8,128)S(1)} %fusion), channel_id=1, source_target_pairs={{0,3},{1,2},{2,1},{3,0},{4,7},{5,6},{6,5},{7,4},{8,11},{9,10},{10,... | collective-permute-start | bytes 98312 | tf_op jit(solution)/shard_map/tp_sum/ppermute | solution.py:315
  75.1 8.1 %collective-permute-start.11 = (f32[64,128]{1,0:T(8,128)S(1)}, f32[64,128]{1,0:T(8,128)S(1)}, u32[]{:S(2)}, u32[]{:S(2)}) collective-permute-start(f32[64,128]{1,0:T(8,128)S(1)} %fusion), channel_id=1, source_target_pairs={{0,2},{1,3},{2,0},{3,1},{4,6},{5,7},{6,4},{7,5},{8,10},{9,11},{10,... | collective-permute-start | bytes 98312 | tf_op jit(solution)/shard_map/tp_sum/ppermute | solution.py:315
  75.5 7.8 %collective-permute-start.10 = (f32[64,128]{1,0:T(8,128)S(1)}, f32[64,128]{1,0:T(8,128)S(1)}, u32[]{:S(2)}, u32[]{:S(2)}) collective-permute-start(f32[64,128]{1,0:T(8,128)S(1)} %fusion), channel_id=1, source_target_pairs={{0,1},{1,0},{2,3},{3,2},{4,5},{5,4},{6,7},{7,6},{8,9},{9,8},{10,11... | collective-permute-start | bytes 98312 | tf_op jit(solution)/shard_map/tp_sum/ppermute | solution.py:315

commit v4 on v3

--- a/solution.py
+++ b/solution.py
@@ -250,16 +250,19 @@
 
 
 def anchor_moves():
-    keys_2 = [[((x, 0), (x + dx, dz)) for x in (0, 2)] for dx, dz in ((1, 0), (0, 3), (1, 3))]
+    keys_2 = [
+        [((0, 0), (dx, dz)), ((3, 0), (3 - dx, dz))] for dx, dz in ((1, 0), (0, 3), (1, 3))
+    ]
     values_2 = [
-        [((0, 0), (dx, -dz % NZ)), ((0, 2), (dx, 2 + dz))] for dx, dz in ((0, 2), (2, 0), (2, 2))
+        [((0, 0), (dx, 6 * dz)), ((0, 1), (dx, 1 + 2 * dz))] for dx, dz in ((0, 1), (2, 0), (2, 1))
     ]
     keys_3 = [
         [((x, 0), (x, near)) for x in range(NX)] + [((x, 3), (x, far)) for x in range(NX)]
         for near, far in ((1, 2), (7, 4), (6, 5))
     ]
     values_3 = [
-        [((x, z), (x + dx, z + dz)) for x in (0, 2) for z in (0, 2, 4, 6)] for dx, dz in ((1, 0), (0, 1), (1, 1))
+        [((x, z), (x + dx, beside if dz else z)) for x in (0, 2) for z, beside in ((0, 7), (1, 2), (3, 4), (6, 5))]
+        for dx, dz in ((1, 0), (0, 1), (1, 1))
     ]
 
     def join(keys, values):
@@ -283,7 +286,7 @@
 
     with jax.named_scope("anchor_step1"):
         root = ctx_at(0, 0, 0)
-        moves = [[(root, ctx_at(2, 0, 0))], [(root, ctx_at(0, 0, 1))], [(root, ctx_at(0, 2, 1))]]
+        moves = [[(root, ctx_at(3, 0, 0))], [(root, ctx_at(0, 0, 1))], [(root, ctx_at(0, 1, 1))]]
         held = place(keys, [perm(block, pairs) for block, pairs in zip((keys, values, values), moves)], moves)
     for number, moves in enumerate(anchor_moves()):
         with jax.named_scope(f"anchor_step{number + 2}"):

time: 84.6 us -> 84.8 us (level)
  transfers between devices with their start and end apart: 17 -> 17, of which waited for: 4 -> 4; matrix products, arithmetic and copies ran while one was open for 1% -> 1% of each run, Pallas kernels for 24% -> 23%
where the time goes in v4:
time: 84.8 us; the launch traced here: 84 us
  starting transfers between devices  48.2 us (57%)
  Pallas kernels  20.5 us (24%)
  waiting for transfers between devices  10.7 us (13%)
  other arithmetic  1.76 us (2%)
  local copies, waits for them, and re-layouts  1.57 us (2%)
  between operations  1.14 us (1%)
    ppermute x10, starting transfers between devices, fetch_anchor(): perm = lambda block, pairs: lax.ppermute(block, 'ctx', pairs)  18.2 us
    pallas_call x2, Pallas kernels, block_pass(): pl.pallas_call(functools.partial(block_kernel, step), grid_spec=pltpu.Pre...  15 us
    all_to_all x1, starting transfers between devices, body(): rows = lax.all_to_all(copies, 'ctx', 0, 0, tiled=True)  12.4 us
    all_to_all x1, waiting for transfers between devices, body(): lax.all_to_all(merged, 'ctx', 0, 0, axis_index_groups=FAR_GROUPS, tiled=T...  6.7 us
    all_to_all x1, starting transfers between devices, body(): lax.all_to_all(attn, 'ctx', 0, 0, axis_index_groups=NEAR_GROUPS, tiled=True)  5.77 us
    all_to_all x1, starting transfers between devices, body(): lax.all_to_all(message, 'ctx', 0, 0, axis_index_groups=NEAR_GROUPS, tiled...  5.01 us
    ppermute x3, starting transfers between devices, body(): lax.ppermute(projected, 'tp', [(i, i ^ k) for i in range(NTP)])  3.51 us
    all_to_all x1, starting transfers between devices, body(): lax.all_to_all(merged, 'ctx', 0, 0, axis_index_groups=FAR_GROUPS, tiled=T...  3.29 us
  transfers between devices with their start and end apart: 17, of which 4 were waited for; matrix products, arithmetic and copies ran while one was open for 1% of the time, Pallas kernels for 23%

profile of v4, /device:TPU:1, one launch (start us, length us, event | category | flops | bytes accessed | tf_op | source)
XLA Modules:
  0.0 84.0 jit_solution(16867489382006722058)
XLA Ops:
  0.6 0.0 copy-start
  0.6 0.0 copy-start.2
  0.7 0.0 copy-start.1
  0.7 0.8 copy-done.3
  1.5 0.7 spread_rows.1
  2.2 1.3 %collective-permute-start.1 = (bf16[512,256]{1,0:T(8,128)(2,1)}, bf16[512,256]{1,0:T(8,128)(2,1)S(1)}, u32[]{:S(2)}, u32[]{:S(2)}) collective-permute-start(bf16[512,256]{1,0:T(8,128)(2,1)} %v_ref.2), channel_id=1, source_target_pairs={{0,4},{1,5},{2,6},{3,7}} | collective-permute-start | bytes 786440 | tf_op jit(solution)/shard_map/anchor_step1/ppermute | solution.py:279
  3.5 0.7 collective-permute-start
  4.2 0.7 collective-permute-start.2
  4.8 12.4 %all-to-all-start = ((bf16[64,16,128]{2,1,0:T(8,128)(2,1)}), bf16[64,16,128]{2,1,0:T(8,128)(2,1)S(1)}, u32[]{:S(2)}, u32[]{:S(2)}) async-start(bf16[64,16,128]{2,1,0:T(8,128)(2,1)} %spread_rows.1), calls=%async_computation | async-start | bytes 524288 | tf_op jit(solution)/shard_map/rows_out/all_to_all | solution.py:305
  17.2 0.0 collective-permute-done.1
  17.2 0.0 collective-permute-done
  17.3 0.0 collective-permute-done.2
  17.3 1.0 %select_select_fusion.2 = bf16[512,256]{1,0:T(8,128)(2,1)S(1)} fusion(bf16[512,256]{1,0:T(8,128)(2,1)S(1)} %collective-permute-done, bf16[512,256]{1,0:T(8,128)(2,1)S(1)} %collective-permute-done.1, bf16[512,256]{1,0:T(8,128)(2,1)S(1)} %collective-permute-done.2, bf16[512,256]{1,0:T(8,128)(2,1)} %k_ref.2, pred[]{:T(512)S(6)} %eq.211, pred[]{:T(512)S(6)} %eq.210, ...), kind=kLoop, calls=%fused_computation.2 | loop fusion | flops 393216 | bytes 1310723 | tf_op jit(solution)/shard_map/anchor_step1/jit(_where)/select_n | solution.py:284
  18.3 5.4 %collective-permute-start.5 = (bf16[512,256]{1,0:T(8,128)(2,1)S(1)}, bf16[512,256]{1,0:T(8,128)(2,1)S(1)}, u32[]{:S(2)}, u32[]{:S(2)}) collective-permute-start(bf16[512,256]{1,0:T(8,128)(2,1)S(1)} %select_select_fusion.2), channel_id=1, source_target_pairs={{0,64},{192,128},{4,52},{12,28},{1,65},{193,129},{5,53},{13,29},{2... | collective-permute-start | bytes 786440 | tf_op jit(solution)/shard_map/anchor_step2/ppermute | solution.py:279
  23.7 1.3 %collective-permute-start.4 = (bf16[512,256]{1,0:T(8,128)(2,1)S(1)}, bf16[512,256]{1,0:T(8,128)(2,1)S(1)}, u32[]{:S(2)}, u32[]{:S(2)}) collective-permute-start(bf16[512,256]{1,0:T(8,128)(2,1)S(1)} %select_select_fusion.2), channel_id=1, source_target_pairs={{0,24},{192,216},{4,132},{12,140},{1,25},{193,217},{5,133},{13,141... | collective-permute-start | bytes 786440 | tf_op jit(solution)/shard_map/anchor_step2/ppermute | solution.py:279
  25.0 2.6 %collective-permute-start.3 = (bf16[512,256]{1,0:T(8,128)(2,1)S(1)}, bf16[512,256]{1,0:T(8,128)(2,1)S(1)}, u32[]{:S(2)}, u32[]{:S(2)}) collective-permute-start(bf16[512,256]{1,0:T(8,128)(2,1)S(1)} %select_select_fusion.2), channel_id=1, source_target_pairs={{0,88},{192,152},{4,180},{12,156},{1,89},{193,153},{5,181},{13,157... | collective-permute-start | bytes 786440 | tf_op jit(solution)/shard_map/anchor_step2/ppermute | solution.py:279
  27.7 1.4 %all-to-all-done.q_ref = bf16[64,16,128]{2,1,0:T(8,128)(2,1)S(1)} async-done(((bf16[64,16,128]{2,1,0:T(8,128)(2,1)}), bf16[64,16,128]{2,1,0:T(8,128)(2,1)S(1)}, u32[]{:S(2)}, u32[]{:S(2)}) %all-to-all-start) | async-done | bytes 262176 | tf_op jit(solution)/shard_map/rows_out/all_to_all | solution.py:305
  29.1 2.8 %decode_part.1 = bf16[16,4,2176]{2,1,0:T(4,128)(2,1)} custom-call(s32[64]{0:T(128)S(1)} %copy-done.4, bf16[64,16,128]{2,1,0:T(8,128)(2,1)S(1)} %all-to-all-done.q_ref, bf16[512,256]{1,0:T(8,128)(2,1)S(1)} %copy-done.1, bf16[512,256]{1,0:T(8,128)(2,1)S(1)} %copy-done.2), custom_call_target="tpu_custom_call" | custom-call | flops 268435456 | bytes 1048576 | tf_op jit(solution)/shard_map/decode_part/pallas_call | solution.py:199
  31.9 5.0 %all-to-all-start.1 = ((bf16[16,4,2176]{2,1,0:T(4,128)(2,1)}), bf16[16,4,2176]{2,1,0:T(4,128)(2,1)S(1)}, u32[]{:S(2)}, u32[]{:S(2)}) async-start(bf16[16,4,2176]{2,1,0:T(4,128)(2,1)} %decode_part.1), calls=%async_computation.1 | async-start | bytes 557056 | tf_op jit(solution)/shard_map/parts_near/all_to_all | solution.py:308
  36.9 0.0 collective-permute-done.5
  36.9 0.0 collective-permute-done.4
  36.9 0.1 select_select_fusion.1
  37.0 3.3 %collective-permute-start.8 = (bf16[512,256]{1,0:T(8,128)(2,1)S(1)}, bf16[512,256]{1,0:T(8,128)(2,1)S(1)}, u32[]{:S(2)}, u32[]{:S(2)}) collective-permute-start(bf16[512,256]{1,0:T(8,128)(2,1)S(1)} %select_select_fusion.1), channel_id=1, source_target_pairs={{0,8},{64,72},{128,136},{192,200},{24,16},{88,80},{152,144},{216,2... | collective-permute-start | bytes 786440 | tf_op jit(solution)/shard_map/anchor_step3/ppermute | solution.py:279
  40.3 1.3 %collective-permute-start.7 = (bf16[512,256]{1,0:T(8,128)(2,1)S(1)}, bf16[512,256]{1,0:T(8,128)(2,1)S(1)}, u32[]{:S(2)}, u32[]{:S(2)}) collective-permute-start(bf16[512,256]{1,0:T(8,128)(2,1)S(1)} %select_select_fusion.1), channel_id=1, source_target_pairs={{0,56},{64,120},{128,184},{192,248},{24,32},{88,96},{152,160},{216... | collective-permute-start | bytes 786440 | tf_op jit(solution)/shard_map/anchor_step3/ppermute | solution.py:279
  41.6 1.3 %collective-permute-start.6 = (bf16[512,256]{1,0:T(8,128)(2,1)S(1)}, bf16[512,256]{1,0:T(8,128)(2,1)S(1)}, u32[]{:S(2)}, u32[]{:S(2)}) collective-permute-start(bf16[512,256]{1,0:T(8,128)(2,1)S(1)} %select_select_fusion.1), channel_id=1, source_target_pairs={{0,48},{64,112},{128,176},{192,240},{24,40},{88,104},{152,168},{21... | collective-permute-start | bytes 786440 | tf_op jit(solution)/shard_map/anchor_step3/ppermute | solution.py:279
  42.9 1.3 %all-to-all-done.1.in_ref = bf16[16,4,2176]{2,1,0:T(4,128)(2,1)S(1)} async-done(((bf16[16,4,2176]{2,1,0:T(4,128)(2,1)}), bf16[16,4,2176]{2,1,0:T(4,128)(2,1)S(1)}, u32[]{:S(2)}, u32[]{:S(2)}) %all-to-all-start.1) | async-done | bytes 278560 | tf_op jit(solution)/shard_map/parts_near/all_to_all | solution.py:308
  44.2 1.0 %merge_parts.2 = bf16[4,4,2176]{2,1,0:T(4,128)(2,1)} custom-call(bf16[16,4,2176]{2,1,0:T(4,128)(2,1)S(1)} %all-to-all-done.1.in_ref), custom_call_target="tpu_custom_call" | custom-call | flops 1048576 | bytes 524288 | tf_op jit(solution)/shard_map/merge_parts/pallas_call | solution.py:241
  45.2 3.3 %all-to-all-start.2 = ((bf16[4,4,2176]{2,1,0:T(4,128)(2,1)}), bf16[4,4,2176]{2,1,0:T(4,128)(2,1)S(1)}, u32[]{:S(2)}, u32[]{:S(2)}) async-start(bf16[4,4,2176]{2,1,0:T(4,128)(2,1)} %merge_parts.2), calls=%async_computation.2 | async-start | bytes 139264 | tf_op jit(solution)/shard_map/parts_far/all_to_all | solution.py:312
  48.7 6.7 %all-to-all-done.2.in_ref = bf16[4,4,2176]{2,1,0:T(4,128)(2,1)S(1)} async-done(((bf16[4,4,2176]{2,1,0:T(4,128)(2,1)}), bf16[4,4,2176]{2,1,0:T(4,128)(2,1)S(1)}, u32[]{:S(2)}, u32[]{:S(2)}) %all-to-all-start.2) | async-done | bytes 69664 | tf_op jit(solution)/shard_map/parts_far/all_to_all | solution.py:312
  55.4 1.0 %merge_parts.3 = bf16[16,4,2048]{2,1,0:T(4,128)(2,1)} custom-call(bf16[4,4,2176]{2,1,0:T(4,128)(2,1)S(1)} %all-to-all-done.2.in_ref), custom_call_target="tpu_custom_call" | custom-call | flops 1048576 | bytes 524288 | tf_op jit(solution)/shard_map/merge_parts/pallas_call | solution.py:241
  56.4 5.8 %all-to-all-start.3 = ((bf16[16,4,2048]{2,1,0:T(4,128)(2,1)}), bf16[16,4,2048]{2,1,0:T(4,128)(2,1)S(1)}, u32[]{:S(2)}, u32[]{:S(2)}) async-start(bf16[16,4,2048]{2,1,0:T(4,128)(2,1)} %merge_parts.3), calls=%async_computation.3 | async-start | bytes 524288 | tf_op jit(solution)/shard_map/attn_near/all_to_all | solution.py:315
  62.2 0.0 collective-permute-done.8
  62.2 0.0 collective-permute-done.6
  62.2 0.1 select_select_fusion.one_ref
  62.3 0.3 collective-permute-start.9
  62.6 1.3 %collective-permute-done.9.two_ref = bf16[512,256]{1,0:T(8,128)(2,1)S(1)} collective-permute-done((bf16[512,256]{1,0:T(8,128)(2,1)S(1)}, bf16[512,256]{1,0:T(8,128)(2,1)S(1)}, u32[]{:S(2)}, u32[]{:S(2)}) %collective-permute-start.9) | collective-permute-done | bytes 262176 | tf_op jit(solution)/shard_map/anchor_swap/ppermute | solution.py:279
  63.9 0.7 copy-done.6
  64.6 7.6 %block_pass.2.rest_0_ = bf16[512,2048]{1,0:T(8,128)(2,1)} custom-call(s32[64]{0:T(128)} %lens.5, bf16[512,2048]{1,0:T(8,128)(2,1)} %q_ref.3, bf16[512,256]{1,0:T(8,128)(2,1)} %k_ref.2, bf16[512,256]{1,0:T(8,128)(2,1)} %v_ref.2, bf16[512,256]{1,0:T(8,128)(2,1)} %copy-done.5, bf16[512,256]{1,0:T(8,128)(2,1)} %copy-done.6), custom_call_target="tpu_custom_call" | custom-call | flops 2147483648 | bytes 4194304 | tf_op jit(solution)/shard_map/block_pass/pallas_call | solution.py:124
  72.2 0.0 all-to-all-done.3
  72.2 0.1 reshape.7
  72.3 0.2 fusion
  72.5 2.8 %collective-permute-start.12 = (f32[64,128]{1,0:T(8,128)S(1)}, f32[64,128]{1,0:T(8,128)S(1)}, u32[]{:S(2)}, u32[]{:S(2)}) collective-permute-start(f32[64,128]{1,0:T(8,128)S(1)} %fusion), channel_id=1, source_target_pairs={{0,3},{1,2},{2,1},{3,0},{4,7},{5,6},{6,5},{7,4},{8,11},{9,10},{10,... | collective-permute-start | bytes 98312 | tf_op jit(solution)/shard_map/tp_sum/ppermute | solution.py:318
  75.3 0.3 collective-permute-start.11
  75.7 0.3 collective-permute-start.10
  76.0 7.4 %block_pass.3 = bf16[512,2048]{1,0:T(8,128)(2,1)} custom-call(s32[64]{0:T(128)} %lens.5, bf16[512,2048]{1,0:T(8,128)(2,1)} %q_ref.3, bf16[512,256]{1,0:T(8,128)(2,1)} %k_ref.2, bf16[512,256]{1,0:T(8,128)(2,1)} %v_ref.2, bf16[512,256]{1,0:T(8,128)(2,1)} %copy-done.5, bf16[512,256]{1,0:T(8,128)(2,1)} %copy-done.6, ...), custom_call_target="tpu_custom_call", output_to_operand_aliasing={{}: (6, {})} | custom-call | flops 2147483648 | bytes 4194304 | tf_op jit(solution)/shard_map/block_pass/pallas_call | solution.py:124
  83.4 0.0 collective-permute-done.11
  83.4 0.0 collective-permute-done.10
  83.4 0.6 add_convert_fusion
  (12 shorter events, 0.0 us)
Async XLA Ops:
  0.6 71.6 %copy-start = (bf16[2048,128]{1,0:T(8,128)(2,1)S(1)}, bf16[2048,128]{1,0:T(8,128)(2,1)}, u32[]{:S(2)}) copy-start(bf16[2048,128]{1,0:T(8,128)(2,1)} %param.11) | copy-start | bytes 1572868
  0.6 28.5 %copy-start.2 = (bf16[512,256]{1,0:T(8,128)(2,1)S(1)}, bf16[512,256]{1,0:T(8,128)(2,1)}, u32[]{:S(2)}) copy-start(bf16[512,256]{1,0:T(8,128)(2,1)} %v_ref.2) | copy-start | bytes 786436
  0.7 28.4 %copy-start.1 = (bf16[512,256]{1,0:T(8,128)(2,1)S(1)}, bf16[512,256]{1,0:T(8,128)(2,1)}, u32[]{:S(2)}) copy-start(bf16[512,256]{1,0:T(8,128)(2,1)} %k_ref.2) | copy-start | bytes 786436
  0.7 0.8 copy-start.3
  1.4 27.7 %copy-start.4 = (s32[64]{0:T(128)S(1)}, s32[64]{0:T(128)}, u32[]{:S(2)}) copy-start(s32[64]{0:T(128)} %lens.5) | copy-start | bytes 772
  2.2 15.1 %collective-permute-start.1 = (bf16[512,256]{1,0:T(8,128)(2,1)}, bf16[512,256]{1,0:T(8,128)(2,1)S(1)}, u32[]{:S(2)}, u32[]{:S(2)}) collective-permute-start(bf16[512,256]{1,0:T(8,128)(2,1)} %v_ref.2), channel_id=1, source_target_pairs={{0,4},{1,5},{2,6},{3,7}} | collective-permute-start | bytes 786440 | tf_op jit(solution)/shard_map/anchor_step1/ppermute | solution.py:279
  3.5 13.8 %collective-permute-start = (bf16[512,256]{1,0:T(8,128)(2,1)}, bf16[512,256]{1,0:T(8,128)(2,1)S(1)}, u32[]{:S(2)}, u32[]{:S(2)}) collective-permute-start(bf16[512,256]{1,0:T(8,128)(2,1)} %v_ref.2), channel_id=1, source_target_pairs={{0,12},{1,13},{2,14},{3,15}} | collective-permute-start | bytes 786440 | tf_op jit(solution)/shard_map/anchor_step1/ppermute | solution.py:279
  4.2 13.1 %collective-permute-start.2 = (bf16[512,256]{1,0:T(8,128)(2,1)}, bf16[512,256]{1,0:T(8,128)(2,1)S(1)}, u32[]{:S(2)}, u32[]{:S(2)}) collective-permute-start(bf16[512,256]{1,0:T(8,128)(2,1)} %k_ref.2), channel_id=1, source_target_pairs={{0,192},{1,193},{2,194},{3,195}} | collective-permute-start | bytes 786440 | tf_op jit(solution)/shard_map/anchor_step1/ppermute | solution.py:279
  4.8 24.3 %all-to-all-start = ((bf16[64,16,128]{2,1,0:T(8,128)(2,1)}), bf16[64,16,128]{2,1,0:T(8,128)(2,1)S(1)}, u32[]{:S(2)}, u32[]{:S(2)}) async-start(bf16[64,16,128]{2,1,0:T(8,128)(2,1)} %spread_rows.1), calls=%async_computation | async-start | bytes 524288 | tf_op jit(solution)/shard_map/rows_out/all_to_all | solution.py:305
  18.3 18.6 %collective-permute-start.5 = (bf16[512,256]{1,0:T(8,128)(2,1)S(1)}, bf16[512,256]{1,0:T(8,128)(2,1)S(1)}, u32[]{:S(2)}, u32[]{:S(2)}) collective-permute-start(bf16[512,256]{1,0:T(8,128)(2,1)S(1)} %select_select_fusion.2), channel_id=1, source_target_pairs={{0,64},{192,128},{4,52},{12,28},{1,65},{193,129},{5,53},{13,29},{2... | collective-permute-start | bytes 786440 | tf_op jit(solution)/shard_map/anchor_step2/ppermute | solution.py:279
  23.7 13.2 %collective-permute-start.4 = (bf16[512,256]{1,0:T(8,128)(2,1)S(1)}, bf16[512,256]{1,0:T(8,128)(2,1)S(1)}, u32[]{:S(2)}, u32[]{:S(2)}) collective-permute-start(bf16[512,256]{1,0:T(8,128)(2,1)S(1)} %select_select_fusion.2), channel_id=1, source_target_pairs={{0,24},{192,216},{4,132},{12,140},{1,25},{193,217},{5,133},{13,141... | collective-permute-start | bytes 786440 | tf_op jit(solution)/shard_map/anchor_step2/ppermute | solution.py:279
  25.0 11.8 %collective-permute-start.3 = (bf16[512,256]{1,0:T(8,128)(2,1)S(1)}, bf16[512,256]{1,0:T(8,128)(2,1)S(1)}, u32[]{:S(2)}, u32[]{:S(2)}) collective-permute-start(bf16[512,256]{1,0:T(8,128)(2,1)S(1)} %select_select_fusion.2), channel_id=1, source_target_pairs={{0,88},{192,152},{4,180},{12,156},{1,89},{193,153},{5,181},{13,157... | collective-permute-start | bytes 786440 | tf_op jit(solution)/shard_map/anchor_step2/ppermute | solution.py:279
  31.9 12.3 %all-to-all-start.1 = ((bf16[16,4,2176]{2,1,0:T(4,128)(2,1)}), bf16[16,4,2176]{2,1,0:T(4,128)(2,1)S(1)}, u32[]{:S(2)}, u32[]{:S(2)}) async-start(bf16[16,4,2176]{2,1,0:T(4,128)(2,1)} %decode_part.1), calls=%async_computation.1 | async-start | bytes 557056 | tf_op jit(solution)/shard_map/parts_near/all_to_all | solution.py:308
  37.0 25.2 %collective-permute-start.8 = (bf16[512,256]{1,0:T(8,128)(2,1)S(1)}, bf16[512,256]{1,0:T(8,128)(2,1)S(1)}, u32[]{:S(2)}, u32[]{:S(2)}) collective-permute-start(bf16[512,256]{1,0:T(8,128)(2,1)S(1)} %select_select_fusion.1), channel_id=1, source_target_pairs={{0,8},{64,72},{128,136},{192,200},{24,16},{88,80},{152,144},{216,2... | collective-permute-start | bytes 786440 | tf_op jit(solution)/shard_map/anchor_step3/ppermute | solution.py:279
  40.3 21.9 %collective-permute-start.7 = (bf16[512,256]{1,0:T(8,128)(2,1)S(1)}, bf16[512,256]{1,0:T(8,128)(2,1)S(1)}, u32[]{:S(2)}, u32[]{:S(2)}) collective-permute-start(bf16[512,256]{1,0:T(8,128)(2,1)S(1)} %select_select_fusion.1), channel_id=1, source_target_pairs={{0,56},{64,120},{128,184},{192,248},{24,32},{88,96},{152,160},{216... | collective-permute-start | bytes 786440 | tf_op jit(solution)/shard_map/anchor_step3/ppermute | solution.py:279
  41.6 20.6 %collective-permute-start.6 = (bf16[512,256]{1,0:T(8,128)(2,1)S(1)}, bf16[512,256]{1,0:T(8,128)(2,1)S(1)}, u32[]{:S(2)}, u32[]{:S(2)}) collective-permute-start(bf16[512,256]{1,0:T(8,128)(2,1)S(1)} %select_select_fusion.1), channel_id=1, source_target_pairs={{0,48},{64,112},{128,176},{192,240},{24,40},{88,104},{152,168},{21... | collective-permute-start | bytes 786440 | tf_op jit(solution)/shard_map/anchor_step3/ppermute | solution.py:279
  45.2 10.3 %all-to-all-start.2 = ((bf16[4,4,2176]{2,1,0:T(4,128)(2,1)}), bf16[4,4,2176]{2,1,0:T(4,128)(2,1)S(1)}, u32[]{:S(2)}, u32[]{:S(2)}) async-start(bf16[4,4,2176]{2,1,0:T(4,128)(2,1)} %merge_parts.2), calls=%async_computation.2 | async-start | bytes 139264 | tf_op jit(solution)/shard_map/parts_far/all_to_all | solution.py:312
  56.4 15.8 %all-to-all-start.3 = ((bf16[16,4,2048]{2,1,0:T(4,128)(2,1)}), bf16[16,4,2048]{2,1,0:T(4,128)(2,1)S(1)}, u32[]{:S(2)}, u32[]{:S(2)}) async-start(bf16[16,4,2048]{2,1,0:T(4,128)(2,1)} %merge_parts.3), calls=%async_computation.3 | async-start | bytes 524288 | tf_op jit(solution)/shard_map/attn_near/all_to_all | solution.py:315
  62.2 1.6 %copy-start.5 = (bf16[512,256]{1,0:T(8,128)(2,1)}, bf16[512,256]{1,0:T(8,128)(2,1)S(1)}, u32[]{:S(2)}) copy-start(bf16[512,256]{1,0:T(8,128)(2,1)S(1)} %select_select_fusion.one_ref) | copy-start | bytes 786436
  62.3 1.6 %collective-permute-start.9 = (bf16[512,256]{1,0:T(8,128)(2,1)S(1)}, bf16[512,256]{1,0:T(8,128)(2,1)S(1)}, u32[]{:S(2)}, u32[]{:S(2)}) collective-permute-start(bf16[512,256]{1,0:T(8,128)(2,1)S(1)} %select_select_fusion.one_ref), channel_id=1, source_target_pairs={{0,4},{4,0},{8,12},{12,8},{16,20},{20,16},{24,28},{28,24},{32,36},... | collective-permute-start | bytes 786440 | tf_op jit(solution)/shard_map/anchor_swap/ppermute | solution.py:279
  63.9 0.7 copy-start.6
  72.5 10.9 %collective-permute-start.12 = (f32[64,128]{1,0:T(8,128)S(1)}, f32[64,128]{1,0:T(8,128)S(1)}, u32[]{:S(2)}, u32[]{:S(2)}) collective-permute-start(f32[64,128]{1,0:T(8,128)S(1)} %fusion), channel_id=1, source_target_pairs={{0,3},{1,2},{2,1},{3,0},{4,7},{5,6},{6,5},{7,4},{8,11},{9,10},{10,... | collective-permute-start | bytes 98312 | tf_op jit(solution)/shard_map/tp_sum/ppermute | solution.py:318
  75.3 8.1 %collective-permute-start.11 = (f32[64,128]{1,0:T(8,128)S(1)}, f32[64,128]{1,0:T(8,128)S(1)}, u32[]{:S(2)}, u32[]{:S(2)}) collective-permute-start(f32[64,128]{1,0:T(8,128)S(1)} %fusion), channel_id=1, source_target_pairs={{0,2},{1,3},{2,0},{3,1},{4,6},{5,7},{6,4},{7,5},{8,10},{9,11},{10,... | collective-permute-start | bytes 98312 | tf_op jit(solution)/shard_map/tp_sum/ppermute | solution.py:318
  75.7 7.8 %collective-permute-start.10 = (f32[64,128]{1,0:T(8,128)S(1)}, f32[64,128]{1,0:T(8,128)S(1)}, u32[]{:S(2)}, u32[]{:S(2)}) collective-permute-start(f32[64,128]{1,0:T(8,128)S(1)} %fusion), channel_id=1, source_target_pairs={{0,1},{1,0},{2,3},{3,2},{4,5},{5,4},{6,7},{7,6},{8,9},{9,8},{10,11... | collective-permute-start | bytes 98312 | tf_op jit(solution)/shard_map/tp_sum/ppermute | solution.py:318
